TPU v7x, 128 devices: a whole 4x4x4 slice. The times are simulated.
128 devices in a mesh: gx: 4 (over z), gy: 4 (over x_hi, core), gz: 8 (over x_lo, y).
Axes of the slice: x: 4 (x_hi: 2, x_lo: 2; x = x_hi * 2 + x_lo), y: 4, z: 4, core: 2. Of those that a mesh axis runs over, the one named last changes fastest.
Arguments:
- coords: float32 [3, 4, 4096, 128], P(None, 'gx', ('gy', 'gz')), may hold values from 0 to 11
- charges: float32 [4, 4096, 128], P('gx', ('gy', 'gz')), may hold values from -1.5 to 1.5
- atom_types: int32 [4, 4096, 128], P('gx', ('gy', 'gz')), may hold values from 0 to 63
- lj_sigma: float32 [64], replicated, may hold values from 2 to 4
- lj_epsilon: float32 [64], replicated, may hold values from 0.02 to 0.25
- tile_list: int32 [4, 4, 8, 2, 512], P('gx', 'gy', 'gz'), may hold values from -1 to 3455, as said below
Outputs:
- forces: float32 [3, 4, 4096, 128], P(None, 'gx', ('gy', 'gz'))
Inputs may be any that keep to these rules, and one draw needn't show every extreme that they name: tile_list[x, y, z, 0, t] is a block of brick (x, y, z) (0 to 127) and tile_list[x, y, z, 1, t] a block of its neighbourhood whose cell touches the home block's cell or is that cell (cell indices differ by at most one along each dimension, counted across brick faces periodically); on each brick the listed tiles come first and the remaining slots hold -1 in both rows; at least 256 tiles are listed on every brick and all 512 on some brick; tiles may repeat.
All inputs are finite; a program needn't handle non-finite values.
Results may differ from a plain program's by a relative error of at most 0.0003.
Values sent between devices are 32-bit elements; how exact they have to be, the bound alone decides.
No kernel may reach another device: no remote copies, remote signals or barrier semaphores. Data moves between devices by JAX's collectives and lax.ppermute only.
A program may use at most 128 MiB of HBM per device.

v0:
```python
import jax
import jax.numpy as jnp
from jax import lax
from jax.sharding import PartitionSpec as P

GRID = 4


cell_edge = 11.0
cutoff = 9.0
soft_core = 16.0
coulomb = 332.0636


def extended(block, sides, width):
    for axis, dim in sides:
        count = lax.axis_size(axis)
        forward = [(i, i + 1) for i in range(count - 1)]
        forward.append((count - 1, 0))
        backward = [(target, source) for source, target in forward]
        low = lax.ppermute(
            lax.slice_in_dim(block, block.shape[dim] - width, None, axis=dim), axis, forward
        )
        high = lax.ppermute(lax.slice_in_dim(block, 0, width, axis=dim), axis, backward)
        block = jnp.concatenate([low, block, high], axis=dim)
    return block


def radial(softened, sigma_pair, eps_pair, charge_pair):
    ratio = sigma_pair * sigma_pair / softened
    cubed = ratio * ratio * ratio
    return 24.0 * eps_pair * (2.0 * cubed * cubed - cubed) / softened + charge_pair / (
        softened * jnp.sqrt(softened)
    )


def tile_forces(home_block, source_block):
    delta = home_block[:3, :, :, None] - source_block[:3, :, None, :]
    dist_sq = jnp.sum(delta * delta, axis=0)
    softened = dist_sq + soft_core
    sigma_pair = 0.5 * (home_block[4][:, :, None] + source_block[4][:, None, :])
    eps_pair = home_block[5][:, :, None] * source_block[5][:, None, :]
    charge_pair = coulomb * home_block[3][:, :, None] * source_block[3][:, None, :]
    limit = jnp.full_like(softened, cutoff * cutoff + soft_core)
    shifted = radial(softened, sigma_pair, eps_pair, charge_pair) - radial(
        limit, sigma_pair, eps_pair, charge_pair
    )
    strength = jnp.where(dist_sq < cutoff * cutoff, shifted, jnp.zeros_like(shifted))
    return jnp.sum(strength[None] * delta, axis=3)


def brick_forces(home_atoms, region, tile_ids):
    count = tile_ids.shape[1]
    group = min(64, count)
    grouped = tile_ids.reshape(2, count // group, group).transpose(1, 0, 2)
    blocks = home_atoms.shape[1]
    rows = jnp.arange(blocks, dtype=jnp.int32)

    def advance(totals, pair_ids):
        home_block = jnp.take(home_atoms, jnp.maximum(pair_ids[0], 0), axis=1)
        source_block = jnp.take(region, jnp.maximum(pair_ids[1], 0), axis=1)
        pushes = tile_forces(home_block, source_block)
        selector = (pair_ids[0][None, :] == rows[:, None]).astype(totals.dtype)
        added = jnp.einsum("bg,cga->cba", selector, pushes, precision=lax.Precision.HIGHEST)
        return (totals + added, None)

    start = jnp.zeros((3,) + home_atoms.shape[1:], home_atoms.dtype)
    return lax.scan(advance, start, grouped)[0]


def cell_corners(dtype, grid, layers):
    block = jnp.arange(grid * grid * layers, dtype=jnp.int32)
    return (
        jnp.stack([block // (grid * layers), block // layers % grid, block % layers]).astype(dtype)
        * cell_edge
    )


def rim_shift(length, inner, dtype):
    index = jnp.arange(length + 2, dtype=jnp.int32)
    return ((index == length + 1).astype(jnp.int32) - (index == 0).astype(jnp.int32)).astype(
        dtype
    ) * (inner * cell_edge)


def per_device(coords, charges, atom_types, lj_sigma, lj_epsilon, tile_list):
    span_y = lax.axis_size("gy")
    span_z = lax.axis_size("gz")
    blocks = coords.shape[2]
    width = coords.shape[3]
    layers = blocks // (GRID * GRID)
    stride = blocks // (span_y * span_z)
    kinds = jnp.arange(lj_sigma.shape[0], dtype=jnp.int32)
    selector = (atom_types[0][:, :, None] == kinds).astype(coords.dtype)
    sigma_atom = jnp.sum(selector * lj_sigma, axis=2)
    root_atom = jnp.sum(selector * jnp.sqrt(lj_epsilon), axis=2)
    atoms = jnp.concatenate([coords[:, 0], charges, sigma_atom[None], root_atom[None]], 0)
    outgoing = atoms.reshape(6, stride, span_y * span_z, width)[:, None]
    arrived = lax.all_to_all(outgoing, ("gy", "gz"), split_axis=3, concat_axis=1, tiled=True)
    home_atoms = arrived.reshape(6, blocks, width)
    corners = cell_corners(coords.dtype, GRID, layers)
    home_atoms = jnp.concatenate([home_atoms[:3] + corners[:, :, None], home_atoms[3:]], 0)
    pairs = tile_list[0, 0, 0]
    cells = home_atoms.reshape(6, GRID, GRID, layers, width)
    padded = extended(cells, (("gx", 1), ("gy", 2), ("gz", 3)), 1)
    shift_x = rim_shift(GRID, GRID, coords.dtype)
    shift_y = rim_shift(GRID, GRID, coords.dtype)
    shift_z = rim_shift(layers, layers, coords.dtype)
    shape_pad = (GRID + 2, GRID + 2, layers + 2)
    shifts = jnp.stack(
        [
            jnp.broadcast_to(shift_x[:, None, None], shape_pad),
            jnp.broadcast_to(shift_y[None, :, None], shape_pad),
            jnp.broadcast_to(shift_z[None, None, :], shape_pad),
        ]
    )
    region = jnp.concatenate([padded[:3] + shifts[..., None], padded[3:]], 0)
    region = region.reshape(6, (GRID + 2) * (GRID + 2) * (layers + 2), width)
    source = jnp.maximum(pairs[1], 0)
    slot = source // blocks
    member = source % blocks
    place_x = member // (GRID * layers) + (slot // 9 - 1) * GRID + 1
    place_y = member // layers % GRID + (slot // 3 % 3 - 1) * GRID + 1
    place_z = member % layers + (slot % 3 - 1) * layers + 1
    placed = (place_x * (GRID + 2) + place_y) * (layers + 2) + place_z
    placed = jnp.where(pairs[1] < 0, 0, placed)
    pairs = jnp.stack([pairs[0], placed])
    totals = brick_forces(home_atoms, region, pairs)
    sending = totals.reshape(3, span_y * span_z, stride, width)[:, :, :, None]
    returned = lax.all_to_all(sending, ("gy", "gz"), split_axis=1, concat_axis=3, tiled=True)
    return returned.reshape(3, 1, blocks, width)


def solution(mesh):
    return jax.shard_map(
        per_device,
        mesh=mesh,
        in_specs=(
            P(None, "gx", ("gy", "gz"), None),
            P("gx", ("gy", "gz"), None),
            P("gx", ("gy", "gz"), None),
            P(),
            P(),
            P("gx", "gy", "gz", None, None),
        ),
        out_specs=P(None, "gx", ("gy", "gz"), None),
        check_vma=False,
    )
```

profile of v0, /device:TPU:1, one launch (start us, length us, event | category | flops | bytes accessed | tf_op | source)
XLA Modules:
  0.0 228.3 jit_solution(3765208653220287667)
XLA Ops:
  0.0 0.7 sqrt.10
  0.7 2.9 %select_reduce_fusion.1 = (f32[128,128]{1,0:T(8,128)S(1)}, f32[128,128]{1,0:T(8,128)S(1)}) fusion(f32[64]{0:T(128)} %param.11, s32[128,128]{1,0:T(8,128)} %bitcast.110, f32[64]{0:T(128)S(1)} %sqrt.10), kind=kLoop, calls=%fused_computation.40 | loop fusion | flops 5210112 | bytes 197120 | tf_op jit(solution)/shard_map/reduce_sum | solution.py:95
  3.6 1.0 pad_maximum_fusion.2
  4.6 1.0 copy.62
  5.6 8.6 %all-to-all-start = ((f32[6,1,4,32,128]{4,2,1,0,3:T(4,128)}), f32[6,1,4,32,128]{4,2,1,0,3:T(4,128)S(1)}, u32[]{:S(2)}, u32[]{:S(2)}) async-start(f32[6,1,4,32,128]{4,2,1,0,3:T(4,128)} %copy.62), calls=%async_computation | async-start | bytes 786432 | tf_op jit(solution)/shard_map/all_to_all | solution.py:99
  14.2 0.7 compare_reduce_fusion
  14.9 0.8 slice_reduce_fusion
  16.4 7.9 %all-to-all-done = f32[6,1,4,32,128]{4,2,1,0,3:T(4,128)S(1)} async-done(((f32[6,1,4,32,128]{4,2,1,0,3:T(4,128)}), f32[6,1,4,32,128]{4,2,1,0,3:T(4,128)S(1)}, u32[]{:S(2)}, u32[]{:S(2)}) %all-to-all-start) | async-done | bytes 393248 | tf_op jit(solution)/shard_map/all_to_all | solution.py:99
  24.6 1.7 collective-permute-start
  26.3 2.2 collective-permute-start.1
  28.5 2.7 %collective-permute-done = f32[6,1,4,8,128]{4,3,2,1,0:T(8,128)S(1)} collective-permute-done((f32[6,1,4,8,128]{4,3,2,1,0:T(8,128)S(1)}, f32[6,1,4,8,128]{4,3,2,1,0:T(8,128)S(1)}, u32[]{:S(2)}, u32[]{:S(2)}) %collective-permute-start) | collective-permute-done | bytes 98336 | tf_op jit(solution)/shard_map/ppermute | solution.py:21
  31.3 1.7 collective-permute-start.2
  33.2 2.0 collective-permute-done.2
  35.1 4.1 %collective-permute-done.3 = f32[6,6,1,8,128]{4,3,2,1,0:T(8,128)S(1)} collective-permute-done((f32[6,6,1,8,128]{4,3,2,1,0:T(8,128)S(1)}, f32[6,6,1,8,128]{4,3,2,1,0:T(8,128)S(1)}, u32[]{:S(2)}, u32[]{:S(2)}) %collective-permute-start.3) | collective-permute-done | bytes 147488 | tf_op jit(solution)/shard_map/ppermute | solution.py:24
  39.6 3.4 %collective-permute-start.5 = (f32[6,6,6,1,128]{4,3,2,1,0:T(1,128)S(1)}, f32[6,6,6,1,128]{4,3,2,1,0:T(1,128)S(1)}, u32[]{:S(2)}, u32[]{:S(2)}) collective-permute-start(f32[6,6,6,1,128]{4,3,2,1,0:T(1,128)S(1)} %get-tuple-element.114), channel_id=1, source_target_pairs={{1,0},{2,1},{3,2},{4,3},{5,4},{6,5},{7,6},{0,7},{9,8},{10,9},{11,1... | collective-permute-start | bytes 331784 | tf_op jit(solution)/shard_map/ppermute | solution.py:24
  43.3 2.7 %collective-permute-done.4 = f32[6,6,6,1,128]{4,3,2,1,0:T(1,128)S(1)} collective-permute-done((f32[6,6,6,1,128]{4,3,2,1,0:T(1,128)S(1)}, f32[6,6,6,1,128]{4,3,2,1,0:T(1,128)S(1)}, u32[]{:S(2)}, u32[]{:S(2)}) %collective-permute-start.4) | collective-permute-done | bytes 110624 | tf_op jit(solution)/shard_map/ppermute | solution.py:21
  46.9 0.7 copy.67
  47.6 165.6 %while.11 = (s32[]{:T(128)}, f32[3,128,128]{1,2,0:T(8,128)S(1)}, s32[8,2,64]{2,0,1:T(8,128)S(1)}, f32[6,128,128]{2,0,1:T(8,128)S(1)}, f32[6,360,128]{2,0,1:T(8,128)S(1)}, /*index=5*/s32[]{:T(128)}, s32[]{:T(128)}) while((s32[]{:T(128)}, f32[3,128,128]{1,2,0:T(8,128)S(1)}, s32[8,2,64]{2,0,1:T(8,128)S(1)}, ...), condition=%wide.region_5.6_spmd.clone, body=%wide.region_2.5_spmd.clone.sunk | while | flops 88271232 | bytes 20722016 | solution.py:68
  49.5 4.1 %fusion.68 = f32[64,128,128]{2,1,0:T(8,128)S(1)} fusion(f32[3,64,128]{2,1,0:T(8,128)S(1)} %copy.77, f32[3,64,128]{2,1,0:T(8,128)S(1)} %copy.78), kind=kLoop, calls=%fused_computation.5.clone.1 | loop fusion | flops 8388608 | bytes 4390912 | tf_op jit(solution)/shard_map/while/body/eval_jaxpr/reduce_sum | solution.py:39
  53.7 6.5 %fusion.71 = f32[64,128,128]{2,1,0:T(8,128)S(1)} fusion(f32[64,128,128]{2,1,0:T(8,128)S(1)} %fusion.68, f32[64,128]{1,0:T(8,128)S(1)} %bitcast.95, f32[64,128]{1,0:T(8,128)S(1)} %bitcast.98, f32[64,128]{1,0:T(8,128)S(1)} %bitcast.96, f32[64,128]{1,0:T(8,128)S(1)} %bitcast.99, f32[64,128]{1,0:T(8,128)S(1)} %bitcast.94, f32[64,128]{1,0:T(8,128)S(1)} %bitcast.97), kind=kLoop, calls=%fused_computation.16.clone.1 | loop fusion | flops 32505856 | bytes 8585216 | tf_op jit(solution)/shard_map/while/body/eval_jaxpr/jit(_where)/select_n | solution.py:48
  60.2 7.7 %fusion.72 = f32[3,64,128]{2,1,0:T(8,128)S(1)} fusion(f32[64,128,128]{2,1,0:T(8,128)S(1)} %fusion.71, f32[3,64,128]{2,1,0:T(8,128)S(1)} %copy.77, f32[3,64,128]{2,1,0:T(8,128)S(1)} %copy.78), kind=kLoop, calls=%fused_computation.6.clone.1 | loop fusion | flops 9412608 | bytes 4489216 | tf_op jit(solution)/shard_map/while/body/eval_jaxpr/reduce_sum | solution.py:49
  68.4 0.6 gather_fusion
  69.3 0.6 gather_fusion.1
  70.2 4.1 %fusion.68 = f32[64,128,128]{2,1,0:T(8,128)S(1)} fusion(f32[3,64,128]{2,1,0:T(8,128)S(1)} %copy.77, f32[3,64,128]{2,1,0:T(8,128)S(1)} %copy.78), kind=kLoop, calls=%fused_computation.5.clone.1 | loop fusion | flops 8388608 | bytes 4390912 | tf_op jit(solution)/shard_map/while/body/eval_jaxpr/reduce_sum | solution.py:39
  74.3 6.5 %fusion.71 = f32[64,128,128]{2,1,0:T(8,128)S(1)} fusion(f32[64,128,128]{2,1,0:T(8,128)S(1)} %fusion.68, f32[64,128]{1,0:T(8,128)S(1)} %bitcast.95, f32[64,128]{1,0:T(8,128)S(1)} %bitcast.98, f32[64,128]{1,0:T(8,128)S(1)} %bitcast.96, f32[64,128]{1,0:T(8,128)S(1)} %bitcast.99, f32[64,128]{1,0:T(8,128)S(1)} %bitcast.94, f32[64,128]{1,0:T(8,128)S(1)} %bitcast.97), kind=kLoop, calls=%fused_computation.16.clone.1 | loop fusion | flops 32505856 | bytes 8585216 | tf_op jit(solution)/shard_map/while/body/eval_jaxpr/jit(_where)/select_n | solution.py:48
  80.9 7.7 %fusion.72 = f32[3,64,128]{2,1,0:T(8,128)S(1)} fusion(f32[64,128,128]{2,1,0:T(8,128)S(1)} %fusion.71, f32[3,64,128]{2,1,0:T(8,128)S(1)} %copy.77, f32[3,64,128]{2,1,0:T(8,128)S(1)} %copy.78), kind=kLoop, calls=%fused_computation.6.clone.1 | loop fusion | flops 9412608 | bytes 4489216 | tf_op jit(solution)/shard_map/while/body/eval_jaxpr/reduce_sum | solution.py:49
  89.1 0.6 gather_fusion
  90.0 0.6 gather_fusion.1
  90.9 4.1 %fusion.68 = f32[64,128,128]{2,1,0:T(8,128)S(1)} fusion(f32[3,64,128]{2,1,0:T(8,128)S(1)} %copy.77, f32[3,64,128]{2,1,0:T(8,128)S(1)} %copy.78), kind=kLoop, calls=%fused_computation.5.clone.1 | loop fusion | flops 8388608 | bytes 4390912 | tf_op jit(solution)/shard_map/while/body/eval_jaxpr/reduce_sum | solution.py:39
  95.0 6.5 %fusion.71 = f32[64,128,128]{2,1,0:T(8,128)S(1)} fusion(f32[64,128,128]{2,1,0:T(8,128)S(1)} %fusion.68, f32[64,128]{1,0:T(8,128)S(1)} %bitcast.95, f32[64,128]{1,0:T(8,128)S(1)} %bitcast.98, f32[64,128]{1,0:T(8,128)S(1)} %bitcast.96, f32[64,128]{1,0:T(8,128)S(1)} %bitcast.99, f32[64,128]{1,0:T(8,128)S(1)} %bitcast.94, f32[64,128]{1,0:T(8,128)S(1)} %bitcast.97), kind=kLoop, calls=%fused_computation.16.clone.1 | loop fusion | flops 32505856 | bytes 8585216 | tf_op jit(solution)/shard_map/while/body/eval_jaxpr/jit(_where)/select_n | solution.py:48
  101.6 7.7 %fusion.72 = f32[3,64,128]{2,1,0:T(8,128)S(1)} fusion(f32[64,128,128]{2,1,0:T(8,128)S(1)} %fusion.71, f32[3,64,128]{2,1,0:T(8,128)S(1)} %copy.77, f32[3,64,128]{2,1,0:T(8,128)S(1)} %copy.78), kind=kLoop, calls=%fused_computation.6.clone.1 | loop fusion | flops 9412608 | bytes 4489216 | tf_op jit(solution)/shard_map/while/body/eval_jaxpr/reduce_sum | solution.py:49
  111.6 4.1 %fusion.68 = f32[64,128,128]{2,1,0:T(8,128)S(1)} fusion(f32[3,64,128]{2,1,0:T(8,128)S(1)} %copy.77, f32[3,64,128]{2,1,0:T(8,128)S(1)} %copy.78), kind=kLoop, calls=%fused_computation.5.clone.1 | loop fusion | flops 8388608 | bytes 4390912 | tf_op jit(solution)/shard_map/while/body/eval_jaxpr/reduce_sum | solution.py:39
  115.7 6.5 %fusion.71 = f32[64,128,128]{2,1,0:T(8,128)S(1)} fusion(f32[64,128,128]{2,1,0:T(8,128)S(1)} %fusion.68, f32[64,128]{1,0:T(8,128)S(1)} %bitcast.95, f32[64,128]{1,0:T(8,128)S(1)} %bitcast.98, f32[64,128]{1,0:T(8,128)S(1)} %bitcast.96, f32[64,128]{1,0:T(8,128)S(1)} %bitcast.99, f32[64,128]{1,0:T(8,128)S(1)} %bitcast.94, f32[64,128]{1,0:T(8,128)S(1)} %bitcast.97), kind=kLoop, calls=%fused_computation.16.clone.1 | loop fusion | flops 32505856 | bytes 8585216 | tf_op jit(solution)/shard_map/while/body/eval_jaxpr/jit(_where)/select_n | solution.py:48
  122.3 7.7 %fusion.72 = f32[3,64,128]{2,1,0:T(8,128)S(1)} fusion(f32[64,128,128]{2,1,0:T(8,128)S(1)} %fusion.71, f32[3,64,128]{2,1,0:T(8,128)S(1)} %copy.77, f32[3,64,128]{2,1,0:T(8,128)S(1)} %copy.78), kind=kLoop, calls=%fused_computation.6.clone.1 | loop fusion | flops 9412608 | bytes 4489216 | tf_op jit(solution)/shard_map/while/body/eval_jaxpr/reduce_sum | solution.py:49
  132.3 4.1 %fusion.68 = f32[64,128,128]{2,1,0:T(8,128)S(1)} fusion(f32[3,64,128]{2,1,0:T(8,128)S(1)} %copy.77, f32[3,64,128]{2,1,0:T(8,128)S(1)} %copy.78), kind=kLoop, calls=%fused_computation.5.clone.1 | loop fusion | flops 8388608 | bytes 4390912 | tf_op jit(solution)/shard_map/while/body/eval_jaxpr/reduce_sum | solution.py:39
  136.4 6.5 %fusion.71 = f32[64,128,128]{2,1,0:T(8,128)S(1)} fusion(f32[64,128,128]{2,1,0:T(8,128)S(1)} %fusion.68, f32[64,128]{1,0:T(8,128)S(1)} %bitcast.95, f32[64,128]{1,0:T(8,128)S(1)} %bitcast.98, f32[64,128]{1,0:T(8,128)S(1)} %bitcast.96, f32[64,128]{1,0:T(8,128)S(1)} %bitcast.99, f32[64,128]{1,0:T(8,128)S(1)} %bitcast.94, f32[64,128]{1,0:T(8,128)S(1)} %bitcast.97), kind=kLoop, calls=%fused_computation.16.clone.1 | loop fusion | flops 32505856 | bytes 8585216 | tf_op jit(solution)/shard_map/while/body/eval_jaxpr/jit(_where)/select_n | solution.py:48
  143.0 7.7 %fusion.72 = f32[3,64,128]{2,1,0:T(8,128)S(1)} fusion(f32[64,128,128]{2,1,0:T(8,128)S(1)} %fusion.71, f32[3,64,128]{2,1,0:T(8,128)S(1)} %copy.77, f32[3,64,128]{2,1,0:T(8,128)S(1)} %copy.78), kind=kLoop, calls=%fused_computation.6.clone.1 | loop fusion | flops 9412608 | bytes 4489216 | tf_op jit(solution)/shard_map/while/body/eval_jaxpr/reduce_sum | solution.py:49
  153.0 4.1 %fusion.68 = f32[64,128,128]{2,1,0:T(8,128)S(1)} fusion(f32[3,64,128]{2,1,0:T(8,128)S(1)} %copy.77, f32[3,64,128]{2,1,0:T(8,128)S(1)} %copy.78), kind=kLoop, calls=%fused_computation.5.clone.1 | loop fusion | flops 8388608 | bytes 4390912 | tf_op jit(solution)/shard_map/while/body/eval_jaxpr/reduce_sum | solution.py:39
  157.1 6.5 %fusion.71 = f32[64,128,128]{2,1,0:T(8,128)S(1)} fusion(f32[64,128,128]{2,1,0:T(8,128)S(1)} %fusion.68, f32[64,128]{1,0:T(8,128)S(1)} %bitcast.95, f32[64,128]{1,0:T(8,128)S(1)} %bitcast.98, f32[64,128]{1,0:T(8,128)S(1)} %bitcast.96, f32[64,128]{1,0:T(8,128)S(1)} %bitcast.99, f32[64,128]{1,0:T(8,128)S(1)} %bitcast.94, f32[64,128]{1,0:T(8,128)S(1)} %bitcast.97), kind=kLoop, calls=%fused_computation.16.clone.1 | loop fusion | flops 32505856 | bytes 8585216 | tf_op jit(solution)/shard_map/while/body/eval_jaxpr/jit(_where)/select_n | solution.py:48
  163.7 7.7 %fusion.72 = f32[3,64,128]{2,1,0:T(8,128)S(1)} fusion(f32[64,128,128]{2,1,0:T(8,128)S(1)} %fusion.71, f32[3,64,128]{2,1,0:T(8,128)S(1)} %copy.77, f32[3,64,128]{2,1,0:T(8,128)S(1)} %copy.78), kind=kLoop, calls=%fused_computation.6.clone.1 | loop fusion | flops 9412608 | bytes 4489216 | tf_op jit(solution)/shard_map/while/body/eval_jaxpr/reduce_sum | solution.py:49
  173.7 4.1 %fusion.68 = f32[64,128,128]{2,1,0:T(8,128)S(1)} fusion(f32[3,64,128]{2,1,0:T(8,128)S(1)} %copy.77, f32[3,64,128]{2,1,0:T(8,128)S(1)} %copy.78), kind=kLoop, calls=%fused_computation.5.clone.1 | loop fusion | flops 8388608 | bytes 4390912 | tf_op jit(solution)/shard_map/while/body/eval_jaxpr/reduce_sum | solution.py:39
  177.8 6.5 %fusion.71 = f32[64,128,128]{2,1,0:T(8,128)S(1)} fusion(f32[64,128,128]{2,1,0:T(8,128)S(1)} %fusion.68, f32[64,128]{1,0:T(8,128)S(1)} %bitcast.95, f32[64,128]{1,0:T(8,128)S(1)} %bitcast.98, f32[64,128]{1,0:T(8,128)S(1)} %bitcast.96, f32[64,128]{1,0:T(8,128)S(1)} %bitcast.99, f32[64,128]{1,0:T(8,128)S(1)} %bitcast.94, f32[64,128]{1,0:T(8,128)S(1)} %bitcast.97), kind=kLoop, calls=%fused_computation.16.clone.1 | loop fusion | flops 32505856 | bytes 8585216 | tf_op jit(solution)/shard_map/while/body/eval_jaxpr/jit(_where)/select_n | solution.py:48
  184.4 7.7 %fusion.72 = f32[3,64,128]{2,1,0:T(8,128)S(1)} fusion(f32[64,128,128]{2,1,0:T(8,128)S(1)} %fusion.71, f32[3,64,128]{2,1,0:T(8,128)S(1)} %copy.77, f32[3,64,128]{2,1,0:T(8,128)S(1)} %copy.78), kind=kLoop, calls=%fused_computation.6.clone.1 | loop fusion | flops 9412608 | bytes 4489216 | tf_op jit(solution)/shard_map/while/body/eval_jaxpr/reduce_sum | solution.py:49
  194.4 4.1 %fusion.68 = f32[64,128,128]{2,1,0:T(8,128)S(1)} fusion(f32[3,64,128]{2,1,0:T(8,128)S(1)} %copy.77, f32[3,64,128]{2,1,0:T(8,128)S(1)} %copy.78), kind=kLoop, calls=%fused_computation.5.clone.1 | loop fusion | flops 8388608 | bytes 4390912 | tf_op jit(solution)/shard_map/while/body/eval_jaxpr/reduce_sum | solution.py:39
  198.5 6.5 %fusion.71 = f32[64,128,128]{2,1,0:T(8,128)S(1)} fusion(f32[64,128,128]{2,1,0:T(8,128)S(1)} %fusion.68, f32[64,128]{1,0:T(8,128)S(1)} %bitcast.95, f32[64,128]{1,0:T(8,128)S(1)} %bitcast.98, f32[64,128]{1,0:T(8,128)S(1)} %bitcast.96, f32[64,128]{1,0:T(8,128)S(1)} %bitcast.99, f32[64,128]{1,0:T(8,128)S(1)} %bitcast.94, f32[64,128]{1,0:T(8,128)S(1)} %bitcast.97), kind=kLoop, calls=%fused_computation.16.clone.1 | loop fusion | flops 32505856 | bytes 8585216 | tf_op jit(solution)/shard_map/while/body/eval_jaxpr/jit(_where)/select_n | solution.py:48
  205.1 7.7 %fusion.72 = f32[3,64,128]{2,1,0:T(8,128)S(1)} fusion(f32[64,128,128]{2,1,0:T(8,128)S(1)} %fusion.71, f32[3,64,128]{2,1,0:T(8,128)S(1)} %copy.77, f32[3,64,128]{2,1,0:T(8,128)S(1)} %copy.78), kind=kLoop, calls=%fused_computation.6.clone.1 | loop fusion | flops 9412608 | bytes 4489216 | tf_op jit(solution)/shard_map/while/body/eval_jaxpr/reduce_sum | solution.py:49
  213.3 14.3 %all_to_all.30 = f32[3,32,4,1,128]{4,2,0,3,1:T(4,128)S(1)} all-to-all(f32[3,32,4,1,128]{4,2,0,3,1:T(4,128)S(1)} %copy.71), channel_id=1, replica_groups=mesh['gx'=4,'gy'=4,'gz'=8] {'gy','gz'}, dimensions={1} | all-to-all | bytes 393216 | tf_op jit(solution)/shard_map/all_to_all | solution.py:130
  227.6 0.7 copy.72
  (163 shorter events, 17.8 us)
Async XLA Ops:
  5.6 18.8 %all-to-all-start = ((f32[6,1,4,32,128]{4,2,1,0,3:T(4,128)}), f32[6,1,4,32,128]{4,2,1,0,3:T(4,128)S(1)}, u32[]{:S(2)}, u32[]{:S(2)}) async-start(f32[6,1,4,32,128]{4,2,1,0,3:T(4,128)} %copy.62), calls=%async_computation | async-start | bytes 786432 | tf_op jit(solution)/shard_map/all_to_all | solution.py:99
  24.6 6.7 %collective-permute-start = (f32[6,1,4,8,128]{4,3,2,1,0:T(8,128)S(1)}, f32[6,1,4,8,128]{4,3,2,1,0:T(8,128)S(1)}, u32[]{:S(2)}, u32[]{:S(2)}) collective-permute-start(f32[6,1,4,8,128]{4,3,2,1,0:T(8,128)S(1)} %get-tuple-element.117), channel_id=1, source_target_pairs={{0,32},{32,64},{64,96},{96,0},{1,33},{33,65},{65,97},{97,1},{2,34}... | collective-permute-start | bytes 294920 | tf_op jit(solution)/shard_map/ppermute | solution.py:21
  26.3 5.0 %collective-permute-start.1 = (f32[6,1,4,8,128]{4,3,2,1,0:T(8,128)S(1)}, f32[6,1,4,8,128]{4,3,2,1,0:T(8,128)S(1)}, u32[]{:S(2)}, u32[]{:S(2)}) collective-permute-start(f32[6,1,4,8,128]{4,3,2,1,0:T(8,128)S(1)} %get-tuple-element.118), channel_id=1, source_target_pairs={{32,0},{64,32},{96,64},{0,96},{33,1},{65,33},{97,65},{1,97},{34,2}... | collective-permute-start | bytes 294920 | tf_op jit(solution)/shard_map/ppermute | solution.py:24
  31.3 3.8 %collective-permute-start.2 = (f32[6,6,1,8,128]{4,3,2,1,0:T(8,128)S(1)}, f32[6,6,1,8,128]{4,3,2,1,0:T(8,128)S(1)}, u32[]{:S(2)}, u32[]{:S(2)}) collective-permute-start(f32[6,6,1,8,128]{4,3,2,1,0:T(8,128)S(1)} %get-tuple-element.115), channel_id=1, source_target_pairs={{0,8},{8,16},{16,24},{24,0},{1,9},{9,17},{17,25},{25,1},{2,10},{10... | collective-permute-start | bytes 442376 | tf_op jit(solution)/shard_map/ppermute | solution.py:21
  33.0 6.2 %collective-permute-start.3 = (f32[6,6,1,8,128]{4,3,2,1,0:T(8,128)S(1)}, f32[6,6,1,8,128]{4,3,2,1,0:T(8,128)S(1)}, u32[]{:S(2)}, u32[]{:S(2)}) collective-permute-start(f32[6,6,1,8,128]{4,3,2,1,0:T(8,128)S(1)} %get-tuple-element.116), channel_id=1, source_target_pairs={{8,0},{16,8},{24,16},{0,24},{9,1},{17,9},{25,17},{1,25},{10,2},{18... | collective-permute-start | bytes 442376 | tf_op jit(solution)/shard_map/ppermute | solution.py:24
  39.4 6.6 %collective-permute-start.4 = (f32[6,6,6,1,128]{4,3,2,1,0:T(1,128)S(1)}, f32[6,6,6,1,128]{4,3,2,1,0:T(1,128)S(1)}, u32[]{:S(2)}, u32[]{:S(2)}) collective-permute-start(f32[6,6,6,1,128]{4,3,2,1,0:T(1,128)S(1)} %get-tuple-element.113), channel_id=1, source_target_pairs={{0,1},{1,2},{2,3},{3,4},{4,5},{5,6},{6,7},{7,0},{8,9},{9,10},{10,1... | collective-permute-start | bytes 331784 | tf_op jit(solution)/shard_map/ppermute | solution.py:21
  39.6 6.4 %collective-permute-start.5 = (f32[6,6,6,1,128]{4,3,2,1,0:T(1,128)S(1)}, f32[6,6,6,1,128]{4,3,2,1,0:T(1,128)S(1)}, u32[]{:S(2)}, u32[]{:S(2)}) collective-permute-start(f32[6,6,6,1,128]{4,3,2,1,0:T(1,128)S(1)} %get-tuple-element.114), channel_id=1, source_target_pairs={{1,0},{2,1},{3,2},{4,3},{5,4},{6,5},{7,6},{0,7},{9,8},{10,9},{11,1... | collective-permute-start | bytes 331784 | tf_op jit(solution)/shard_map/ppermute | solution.py:24
where the time goes:
time: 229 us; the launch traced here: 228 us
  other arithmetic  157 us (69%)
  waiting for transfers between devices  19.5 us (9%)
  starting transfers between devices  17.9 us (8%)
  local copies, waits for them, and re-layouts  15.4 us (7%)
  blocking collectives  14.3 us (6%)
  matrix products  3.16 us (1%)
    reduce_sum x8, other arithmetic, tile_forces(): return jnp.sum(strength[None] * delta, axis=3)  61.2 us
    select_n x8, other arithmetic, tile_forces(): jnp.where(dist_sq < cutoff * cutoff, shifted, jnp.zeros_like(shifted))  52.3 us
    reduce_sum x8, other arithmetic, tile_forces(): dist_sq = jnp.sum(delta * delta, axis=0)  33.1 us
    all_to_all x1, blocking collectives, per_device(): lax.all_to_all(sending, ('gy', 'gz'), split_axis=1, concat_axis=3, tiled=...  14.3 us
    all_to_all x1, starting transfers between devices, per_device(): lax.all_to_all(outgoing, ('gy', 'gz'), split_axis=3, concat_axis=1, tiled...  8.59 us
    all_to_all x1, waiting for transfers between devices, per_device(): lax.all_to_all(outgoing, ('gy', 'gz'), split_axis=3, concat_axis=1, tiled...  7.92 us
    ppermute x3, waiting for transfers between devices, extended(): lax.ppermute(lax.slice_in_dim(block, block.shape[dim] - width, None, axis...  7.43 us
    ppermute x3, starting transfers between devices, extended(): lax.ppermute(lax.slice_in_dim(block, 0, width, axis=dim), axis, backward)  5.64 us
  transfers between devices with their start and end apart: 7, of which 5 were waited for; matrix products, arithmetic and copies ran while one was open for 1% of the time, Pallas kernels for 0%

commit v1 on v0

v1 whole, which is shorter than its diff:
```python
import math

import jax
import jax.numpy as jnp
import numpy as np
from jax import lax
from jax.experimental import pallas as pl
from jax.experimental.pallas import tpu as pltpu
from jax.sharding import PartitionSpec as P

F32 = jnp.float32
BF16 = jnp.bfloat16

GRID = 4
LAYERS = 8
CELL = 11.0
LIMIT = 97.0
COULOMB = 332.0636

ROW_X, ROW_Y, ROW_Z, ROW_C, ROW_TYPE, ROW_Q, ROW_ONE, ROW_CC = range(8)
TYPES = 64
ORDER = 13
NX = 32
NY = 48
NZ = TYPES + 32
BATCH = 4


def placements():
    home = np.zeros((32, NX), np.float32)
    src_w = np.zeros((NX, 32), np.float32)
    src_c = np.zeros((NX, 32), np.float32)
    at = 0

    def term(row, part):
        return part * 8 + row

    for row in (ROW_X, ROW_Y, ROW_Z):
        for i, j in ((0, 0), (0, 1), (1, 0), (1, 1), (0, 2), (2, 0)):
            home[term(row, i), at] = 1.0
            src_w[at, term(row, j)] = -2.0
            at += 1
    for part in range(3):
        home[term(ROW_Q, part), at] = 1.0
        src_w[at, term(ROW_ONE, 0)] = 1.0
        at += 1
    for part in range(3):
        home[term(ROW_ONE, 0), at] = 1.0
        src_w[at, term(ROW_Q, part)] = 1.0
        at += 1
    home[term(ROW_ONE, 0), at] = 1.0
    src_w[at, term(ROW_ONE, 0)] = 16.0
    at += 1
    for i, j in ((0, 0), (0, 1), (1, 0), (1, 1), (0, 2), (2, 0)):
        home[term(ROW_CC, i), at] = 1.0
        src_c[at, term(ROW_C, j)] = 1.0
        at += 1
    place_r = np.zeros((16, 32), np.float32)
    for k, row in enumerate((ROW_X, ROW_Y, ROW_Z)):
        for part in range(3):
            place_r[3 * k + part, term(row, part)] = 1.0
    place_r[9, term(ROW_ONE, 0)] = 1.0
    return home, src_w, src_c, place_r


def weights(lj_sigma, lj_epsilon):
    root = jnp.sqrt(lj_epsilon)
    half = 0.5 * lj_sigma
    powers = [jnp.ones_like(half)]
    for _ in range(ORDER - 1):
        powers.append(powers[-1] * half)

    def halves(table):
        high = lax.reduce_precision(table, 8, 7)
        return high, table - high

    h_high, h_low = halves(jnp.stack([root * p for p in powers]))
    zero = jnp.zeros_like(half)
    p12 = jnp.stack([root * powers[12 - k] * (48.0 * math.comb(12, k)) for k in range(ORDER)])
    p6 = jnp.stack(
        [root * powers[6 - k] * (24.0 * math.comb(6, k)) if k <= 6 else zero for k in range(ORDER)]
    )
    pad = jnp.zeros((NY - 3 * ORDER, TYPES), F32)
    home_y = jnp.concatenate([h_high, h_high, h_low, pad])
    src_y = []
    for table in (p12, p6):
        high, low = halves(table)
        src_y += [high, low, high, pad]
    home_x, src_w, src_c, place_r = placements()
    home = jnp.zeros((NZ, 256), F32)
    home = home.at[TYPES:, :NX].set(home_x).at[:TYPES, 128 : 128 + NY].set(home_y.T)
    fixed = jnp.concatenate([jnp.zeros((2 * NX + 16, TYPES)), np.concatenate([src_w, src_c, place_r])], 1)
    lj = jnp.concatenate([jnp.concatenate(src_y), jnp.zeros((2 * NY, 32), F32)], 1)
    source = jnp.concatenate([fixed, lj])
    return home.astype(BF16), source.astype(BF16)


def unpack_kernel(arrived, out):
    row = lax.broadcasted_iota(jnp.int32, (8, 128), 0)

    def body(s, carry):
        rows = arrived[s]
        cell_x, cell_y, cell_z = s // 8, s // 2 % 4, s % 2 * 4
        for k in range(4):
            block = jnp.concatenate([rows[5 * k : 5 * k + 5], jnp.zeros((3, 128), F32)])
            off_x = cell_x.astype(F32) * CELL - 2 * CELL
            off_y = cell_y.astype(F32) * CELL - 2 * CELL
            off_z = (cell_z + k).astype(F32) * CELL - 4 * CELL
            off = jnp.where(row == ROW_X, off_x, 0.0) + jnp.where(row == ROW_Y, off_y, 0.0)
            out[4 * s + k] = block + (off + jnp.where(row == ROW_Z, off_z, 0.0))
        return carry

    lax.fori_loop(0, 32, body, 0)


def powers_of(w):
    u = lax.rsqrt(w)
    inv = u * u
    inv2 = inv * inv
    inv4 = inv2 * inv2
    return inv4 * (inv2 * inv), inv4, u * inv


def pair_kernel(steps, ids, own, region, w_home, w_src, out, lx, ly, rx, ry, rr, acc, buf_a, buf_b):
    row = lax.broadcasted_iota(jnp.int32, (8, 128), 0)
    kind = lax.broadcasted_iota(jnp.int32, (TYPES, 128), 0)

    def factors(block, off_x, off_y, off_z):
        off = jnp.where(row == ROW_X, off_x, 0.0) + jnp.where(row == ROW_Y, off_y, 0.0)
        moved = block + (off + jnp.where(row == ROW_Z, off_z, 0.0))
        square = jnp.sum(jnp.where(row < 3, moved * moved, 0.0), axis=0, keepdims=True)
        moved = jnp.where(row == ROW_Q, square, jnp.where(row == ROW_ONE, 1.0, moved))
        moved = jnp.where(row == ROW_CC, COULOMB * block[ROW_C : ROW_C + 1], moved)
        high = moved.astype(BF16).astype(F32)
        rest = moved - high
        mid = rest.astype(BF16).astype(F32)
        hot = jnp.where(block[ROW_TYPE : ROW_TYPE + 1].astype(jnp.int32) == kind, 1.0, 0.0)
        return jnp.concatenate([hot, high, mid, rest - mid, jnp.zeros((8, 128), F32)]).astype(BF16)

    def prepare_source(p, carry):
        px, py, pz = p // 60, p // 10 % 6, p % 10

        def off(at, length, span):
            side = (at == length + 1).astype(F32) - (at == 0).astype(F32)
            return side * span

        z = factors(region[p], off(px, 4, 44.0), off(py, 4, 44.0), off(pz, 8, 88.0))
        made = jnp.dot(w_src[...], z, preferred_element_type=F32).astype(BF16)
        rx[p, :, :128] = made[:NX]
        rx[p, :, 128:] = made[NX : 2 * NX]
        rr[p, :, :128] = made[2 * NX : 2 * NX + 16]
        rr[p, :, 128:] = made[2 * NX : 2 * NX + 16]
        at = 2 * NX + 16
        ry[p, :, :128] = made[at : at + NY]
        ry[p, :, 128:] = made[at + NY :]
        return carry

    def prepare_home(b, carry):
        z = factors(own[b], 0.0, 0.0, 0.0)
        made = lax.dot_general(z, w_home[...], (((0,), (0,)), ((), ())), preferred_element_type=F32)
        lx[b] = made[:, :128].astype(BF16)
        ly[b] = made[:, 128:].astype(BF16)
        return carry

    lax.fori_loop(0, 360, prepare_source, 0, unroll=4)
    lax.fori_loop(0, 128, prepare_home, 0, unroll=4)
    acc[...] = jnp.zeros_like(acc)
    k7, k4, k3 = powers_of(jnp.full((8, 128), LIMIT, F32))

    def quantities(buf, batch):
        for q in range(BATCH):
            h, j = ids[0, batch * BATCH + q], ids[1, batch * BATCH + q]
            buf[q, 0] = jnp.dot(lx[h][:, :NX], rx[j], preferred_element_type=F32)
            buf[q, 1] = jnp.dot(ly[h][:, :NY], ry[j], preferred_element_type=F32)

    def forces(buf, batch):
        for q in range(BATCH):
            j, h = ids[1, batch * BATCH + q], ids[2, batch * BATCH + q]

            def part(i, side):
                return buf[q, i, :, 128 * side : 128 * side + 128].reshape(16, 8, 128)

            p7, p4, p3 = powers_of(jnp.minimum(part(0, 0), LIMIT))
            push = (p7 - k7) * part(1, 0) - (p4 - k4) * part(1, 1) + (p3 - k3) * part(0, 1)
            push = push.reshape(128, 128)
            high = push.astype(BF16)
            low = (push - high.astype(F32)).astype(BF16)
            acc[h] += lax.dot_general(
                rr[j],
                jnp.concatenate([high, low], 1),
                (((1,), (1,)), ((), ())),
                preferred_element_type=F32,
            )

    pairs = steps[0]
    quantities(buf_a, 0)

    def body(i, carry):
        quantities(buf_b, 2 * i + 1)
        forces(buf_a, 2 * i)
        quantities(buf_a, jnp.minimum(2 * i + 2, 2 * pairs - 1))
        forces(buf_b, 2 * i + 1)
        return carry

    lax.fori_loop(0, pairs, body, 0)
    total = acc[:128, 9]
    for c in range(3):
        weighed = acc[:128, 3 * c] + acc[:128, 3 * c + 1] + acc[:128, 3 * c + 2]
        out[c] = own[:, c] * total - weighed


def extended(block, sides):
    for axis, dim in sides:
        count = lax.axis_size(axis)
        forward = [(i, (i + 1) % count) for i in range(count)]
        backward = [(target, source) for source, target in forward]
        low = lax.ppermute(
            lax.slice_in_dim(block, block.shape[dim] - 1, None, axis=dim), axis, forward
        )
        high = lax.ppermute(lax.slice_in_dim(block, 0, 1, axis=dim), axis, backward)
        block = jnp.concatenate([low, block, high], axis=dim)
    return block


def per_device(coords, charges, atom_types, lj_sigma, lj_epsilon, tile_list):
    blocks, width = coords.shape[2], coords.shape[3]
    peers = lax.axis_size("gy") * lax.axis_size("gz")
    rows = jnp.concatenate([coords[:, 0], charges, atom_types.astype(F32)], 0)
    outgoing = rows.reshape(5, 4, peers, width).transpose(2, 1, 0, 3).reshape(peers, 20, width)
    arrived = lax.all_to_all(outgoing, ("gy", "gz"), split_axis=0, concat_axis=0, tiled=True)
    own = pl.pallas_call(
        unpack_kernel,
        out_shape=jax.ShapeDtypeStruct((blocks, 8, width), F32),
    )(arrived)
    region = extended(
        own.reshape(GRID, GRID, LAYERS, 8, width), (("gx", 0), ("gy", 1), ("gz", 2))
    ).reshape(360, 8, width)

    home, source = tile_list[0, 0, 0, 0], tile_list[0, 0, 0, 1]
    slot, member = source // blocks, source % blocks
    place_x = member // (GRID * LAYERS) + (slot // 9 - 1) * GRID + 1
    place_y = member // LAYERS % GRID + (slot // 3 % 3 - 1) * GRID + 1
    place_z = member % LAYERS + (slot % 3 - 1) * LAYERS + 1
    place = (place_x * (GRID + 2) + place_y) * (LAYERS + 2) + place_z
    listed = home >= 0
    ids = jnp.stack(
        [jnp.maximum(home, 0), jnp.where(listed, place, 0), jnp.where(listed, home, blocks)]
    )
    count = jnp.sum(listed.astype(jnp.int32))
    steps = ((count + 2 * BATCH - 1) // (2 * BATCH)).reshape(1)
    w_home, w_src = weights(lj_sigma, lj_epsilon)

    vmem = pl.BlockSpec(memory_space=pltpu.VMEM)
    smem = pl.BlockSpec(memory_space=pltpu.SMEM)
    totals = pl.pallas_call(
        pair_kernel,
        out_shape=jax.ShapeDtypeStruct((3, blocks, width), F32),
        in_specs=[smem, smem, vmem, vmem, vmem, vmem],
        out_specs=vmem,
        scratch_shapes=[
            pltpu.VMEM((blocks, 128, 128), BF16),
            pltpu.VMEM((blocks, 128, 128), BF16),
            pltpu.VMEM((360, NX, 256), BF16),
            pltpu.VMEM((360, NY, 256), BF16),
            pltpu.VMEM((360, 16, 256), BF16),
            pltpu.VMEM((blocks + 8, 16, 128), F32),
            pltpu.VMEM((BATCH, 2, 128, 256), F32),
            pltpu.VMEM((BATCH, 2, 128, 256), F32),
        ],
        compiler_params=pltpu.CompilerParams(vmem_limit_bytes=48 << 20),
    )(steps, ids, own, region, w_home, w_src)
    sending = totals.reshape(3, peers, 4, width).transpose(1, 0, 2, 3).reshape(peers, 12, width)
    back = lax.all_to_all(sending, ("gy", "gz"), split_axis=0, concat_axis=0, tiled=True)
    return back.reshape(peers, 3, 4, width).transpose(1, 2, 0, 3).reshape(3, 1, blocks, width)


def solution(mesh):
    return jax.shard_map(
        per_device,
        mesh=mesh,
        in_specs=(
            P(None, "gx", ("gy", "gz"), None),
            P("gx", ("gy", "gz"), None),
            P("gx", ("gy", "gz"), None),
            P(),
            P(),
            P("gx", "gy", "gz", None, None),
        ),
        out_specs=P(None, "gx", ("gy", "gz"), None),
        check_vma=False,
    )
```

time: 229 us -> 142 us (0.62)
  other arithmetic: 157 us -> 6.47 us
  Pallas kernels: 0 us -> 75.9 us
  local copies, waits for them, and re-layouts: 15.4 us -> 7.28 us
  matrix products: 3.16 us -> 0 us
    reduce_sum x17 -> x1, other arithmetic: 97.2 us -> 0.64 us  [per_device(): count = jnp.sum(listed.astype(jnp.int32))]
    pallas_call x0 -> x2, Pallas kernels: none -> 75.9 us  [the longest x1 73.4 us: per_device(): pl.pallas_call(pair_kernel, out_shape=jax.ShapeDtypeStruct((3, blocks, wi...]
    select_n x29 -> x0, other arithmetic: 54.6 us -> none  [the longest x8 52.3 us: tile_forces(): jnp.where(dist_sq < cutoff * cutoff, shifted, jnp.zeros_like(shifted))]
    gather x16 -> x0, local copies, waits for them, and re-layouts: 10.1 us -> none  [the longest x8 5.04 us: advance(): source_block = jnp.take(region, jnp.maximum(pair_ids[1], 0), axis=1)]
    dot_general x8 -> x0, matrix products: 3.16 us -> none  [advance(): jnp.einsum('bg,cga->cba', selector, pushes, precision=lax.Precision.HIGHEST)]
    another operation x1 -> x10, other arithmetic: 0.01 us -> 2.72 us  [per_device(): jnp.stack([jnp.broadcast_to(shift_x[:, None, None], shape_pad), jnp.broad...]
  transfers between devices with their start and end apart: 7 -> 7, of which waited for: 5 -> 5; matrix products, arithmetic and copies ran while one was open for 1% -> 5% of each run, Pallas kernels for 0% -> 0%
where the time goes in v1:
time: 142 us
  Pallas kernels  75.9 us (53%)
  waiting for transfers between devices  18.5 us (13%)
  starting transfers between devices  17.4 us (12%)
  blocking collectives  15.6 us (11%)
  local copies, waits for them, and re-layouts  7.28 us (5%)
  other arithmetic  6.47 us (5%)
    pallas_call x1, Pallas kernels, per_device(): pl.pallas_call(pair_kernel, out_shape=jax.ShapeDtypeStruct((3, blocks, wi...  73.4 us
    all_to_all x1, blocking collectives, per_device(): lax.all_to_all(sending, ('gy', 'gz'), split_axis=0, concat_axis=0, tiled=...  15.6 us
    all_to_all x1, starting transfers between devices, per_device(): lax.all_to_all(outgoing, ('gy', 'gz'), split_axis=0, concat_axis=0, tiled...  8.73 us
    ppermute x3, starting transfers between devices, extended(): high = lax.ppermute(lax.slice_in_dim(block, 0, 1, axis=dim), axis, backward)  6.7 us
    ppermute x3, waiting for transfers between devices, extended(): high = lax.ppermute(lax.slice_in_dim(block, 0, 1, axis=dim), axis, backward)  6.56 us
    all_to_all x1, waiting for transfers between devices, per_device(): lax.all_to_all(outgoing, ('gy', 'gz'), split_axis=0, concat_axis=0, tiled...  6.22 us
    ppermute x3, waiting for transfers between devices, extended(): lax.ppermute(lax.slice_in_dim(block, block.shape[dim] - 1, None, axis=dim...  5.72 us
  transfers between devices with their start and end apart: 7, of which 5 were waited for; matrix products, arithmetic and copies ran while one was open for 5% of the time, Pallas kernels for 0%

profile of v1, /device:TPU:1, one launch (start us, length us, event | category | flops | bytes accessed | tf_op | source)
XLA Modules:
  0.0 142.1 jit_solution(1671705224758324365)
XLA Ops:
  0.0 0.0 copy-start.5
  0.0 0.0 copy-start.6
  0.0 0.9 convert_element_type.12
  0.9 1.0 maximum_bitcast_fusion
  1.9 0.9 copy.72
  2.9 8.7 %all-to-all-start = ((f32[32,20,128]{2,1,0:T(8,128)}), f32[32,20,128]{2,1,0:T(8,128)S(1)}, u32[]{:S(2)}, u32[]{:S(2)}) async-start(f32[32,20,128]{2,1,0:T(8,128)} %copy.72), calls=%async_computation | async-start | bytes 786432 | tf_op jit(solution)/shard_map/all_to_all | solution.py:230
  11.6 0.0 copy-done.5
  11.6 0.0 copy-done.6
  11.7 0.1 stack.134
  11.8 0.1 copy.73
  11.9 0.0 copy-done.2
  11.9 0.1 copy.75
  12.0 0.0 copy-done.7
  12.0 0.6 and_reduce_fusion
  12.7 0.1 pad.18.clone
  12.8 0.1 stack.158
  12.9 0.7 fusion.23
  13.6 2.0 %fusion.2 = bf16[64,48]{1,0:T(8,128)(2,1)S(1)} fusion(bf16[13,64]{0,1:T(8,128)(2,1)S(1)} %sub.57, f32[13,64]{0,1:T(8,128)S(1)} %copy.75, bf16[96,256]{1,0:T(8,128)(2,1)S(1)} %copy.83, s32[]{:T(128)} %bitcast.26, s32[]{:T(128)} %bitcast.27, bf16[48]{0:T(256)(128)(2,1)S(1)} %pad.18.clone, pred[]{:T(512)} %and_reduce_fusion), kind=kLoop, calls=%fused_computation.14 | loop fusion | flops 27648 | bytes 17385 | tf_op jit(solution)/shard_map/select.3
  15.6 6.2 %all-to-all-done.arrived = f32[32,20,128]{2,1,0:T(8,128)S(1)} async-done(((f32[32,20,128]{2,1,0:T(8,128)}), f32[32,20,128]{2,1,0:T(8,128)S(1)}, u32[]{:S(2)}, u32[]{:S(2)}) %all-to-all-start) | async-done | bytes 327712 | tf_op jit(solution)/shard_map/all_to_all | solution.py:230
  21.8 0.8 copy-done.1
  22.6 2.5 %shard_map.82.own = f32[128,8,128]{2,1,0:T(8,128)} custom-call(f32[32,20,128]{2,1,0:T(8,128)} %copy-done.1), custom_call_target="tpu_custom_call" | custom-call | tf_op jit(solution)/shard_map/pallas_call | solution.py:231
  25.1 1.0 fusion.22
  26.1 0.0 copy-start.3
  26.1 3.8 %collective-permute-start.1 = (f32[1,4,8,8,128]{4,3,2,1,0:T(8,128)S(1)}, f32[1,4,8,8,128]{4,3,2,1,0:T(8,128)S(1)}, u32[]{:S(2)}, u32[]{:S(2)}) collective-permute-start(f32[1,4,8,8,128]{4,3,2,1,0:T(8,128)S(1)} %bitcast.117), channel_id=1, source_target_pairs={{32,0},{64,32},{96,64},{0,96},{33,1},{65,33},{97,65},{1,97},{34,2}... | collective-permute-start | bytes 393224 | tf_op jit(solution)/shard_map/ppermute | solution.py:220
  29.9 0.0 collective-permute-start
  30.0 0.0 copy-done.4
  30.0 0.6 fusion.7
  30.6 1.8 %collective-permute-done.1 = f32[1,4,8,8,128]{4,3,2,1,0:T(8,128)S(1)} collective-permute-done((f32[1,4,8,8,128]{4,3,2,1,0:T(8,128)S(1)}, f32[1,4,8,8,128]{4,3,2,1,0:T(8,128)S(1)}, u32[]{:S(2)}, u32[]{:S(2)}) %collective-permute-start.1) | collective-permute-done | bytes 131104 | tf_op jit(solution)/shard_map/ppermute | solution.py:220
  32.4 3.1 %collective-permute-done = f32[1,4,8,8,128]{4,3,2,1,0:T(8,128)S(1)} collective-permute-done((f32[1,4,8,8,128]{4,3,2,1,0:T(8,128)S(1)}, f32[1,4,8,8,128]{4,3,2,1,0:T(8,128)S(1)}, u32[]{:S(2)}, u32[]{:S(2)}) %collective-permute-start) | collective-permute-done | bytes 131104 | tf_op jit(solution)/shard_map/ppermute | solution.py:217
  35.5 1.0 pad_maximum_fusion.3
  36.5 1.6 %collective-permute-start.3 = (f32[6,1,8,8,128]{4,3,2,1,0:T(8,128)S(1)}, f32[6,1,8,8,128]{4,3,2,1,0:T(8,128)S(1)}, u32[]{:S(2)}, u32[]{:S(2)}) collective-permute-start(f32[6,1,8,8,128]{4,3,2,1,0:T(8,128)S(1)} %get-tuple-element.42), channel_id=1, source_target_pairs={{8,0},{16,8},{24,16},{0,24},{9,1},{17,9},{25,17},{1,25},{10,2},{18... | collective-permute-start | bytes 589832 | tf_op jit(solution)/shard_map/ppermute | solution.py:220
  38.1 1.7 %collective-permute-start.2 = (f32[6,1,8,8,128]{4,3,2,1,0:T(8,128)S(1)}, f32[6,1,8,8,128]{4,3,2,1,0:T(8,128)S(1)}, u32[]{:S(2)}, u32[]{:S(2)}) collective-permute-start(f32[6,1,8,8,128]{4,3,2,1,0:T(8,128)S(1)} %get-tuple-element.41), channel_id=1, source_target_pairs={{0,8},{8,16},{16,24},{24,0},{1,9},{9,17},{17,25},{25,1},{2,10},{10... | collective-permute-start | bytes 589832 | tf_op jit(solution)/shard_map/ppermute | solution.py:217
  39.8 0.1 bitcast_maximum_fusion
  39.9 4.7 %collective-permute-done.3 = f32[6,1,8,8,128]{4,3,2,1,0:T(8,128)S(1)} collective-permute-done((f32[6,1,8,8,128]{4,3,2,1,0:T(8,128)S(1)}, f32[6,1,8,8,128]{4,3,2,1,0:T(8,128)S(1)}, u32[]{:S(2)}, u32[]{:S(2)}) %collective-permute-start.3) | collective-permute-done | bytes 196640 | tf_op jit(solution)/shard_map/ppermute | solution.py:220
  44.7 0.0 collective-permute-done.2
  44.7 0.0 copy-done
  44.7 1.3 collective-permute-start.5
  46.0 0.3 collective-permute-start.4
  46.9 1.7 %scatter.9.w_home = bf16[96,256]{1,0:T(8,128)(2,1)S(1)} dynamic-update-slice(bf16[96,256]{1,0:T(8,128)(2,1)S(1)} %copy.83, bf16[64,48]{1,0:T(8,128)(2,1)S(1)} %fusion.2, s32[]{:T(128)} %bitcast.26, s32[]{:T(128)} %bitcast.27) | dynamic-update-slice | bytes 12292 | tf_op jit(solution)/shard_map/scatter | solution.py:91
  48.6 0.7 concatenate.49
  49.4 0.0 copy-done.3
  49.4 0.0 collective-permute-done.5
  49.4 2.6 %collective-permute-done.4 = f32[6,6,1,8,128]{4,3,2,1,0:T(8,128)S(1)} collective-permute-done((f32[6,6,1,8,128]{4,3,2,1,0:T(8,128)S(1)}, f32[6,6,1,8,128]{4,3,2,1,0:T(8,128)S(1)}, u32[]{:S(2)}, u32[]{:S(2)}) %collective-permute-start.4) | collective-permute-done | bytes 147488 | tf_op jit(solution)/shard_map/ppermute | solution.py:217
  52.1 0.1 pad_maximum_fusion
  52.2 73.4 %shard_map.83 = f32[3,128,128]{2,1,0:T(8,128)S(1)} custom-call(s32[1]{0:T(128)} %bitcast.steps, s32[3,512]{1,0:T(4,128)S(1)} %pad_add_fusion.ids, f32[128,8,128]{2,1,0:T(8,128)S(1)} %copy-done, f32[360,8,128]{2,1,0:T(8,128)S(1)} %bitcast.110, bf16[96,256]{1,0:T(8,128)(2,1)S(1)} %scatter.9.w_home, bf16[176,96]{1,0:T(8,128)(2,1)S(1)} %fusion.1.w_src), custom_call_target="tpu_custom_call" | custom-call | tf_op jit(solution)/shard_map/pallas_call | solution.py:255
  125.6 0.1 copy.78
  125.7 15.6 %all_to_all.10 = f32[32,12,128]{2,1,0:T(8,128)S(1)} all-to-all(f32[32,12,128]{2,1,0:T(8,128)S(1)} %copy.78), channel_id=1, replica_groups=mesh['gx'=4,'gy'=4,'gz'=8] {'gy','gz'}, dimensions={0} | all-to-all | bytes 393216 | tf_op jit(solution)/shard_map/all_to_all | solution.py:273
  141.4 0.7 copy.79
  (25 shorter events, 0.2 us)
Async XLA Ops:
  0.0 11.6 %copy-start.5 = (f32[64]{0:T(128)S(1)}, f32[64]{0:T(128)}, u32[]{:S(2)}) copy-start(f32[64]{0:T(128)} %param.16) | copy-start | bytes 772
  0.0 11.6 %copy-start.6 = (f32[64]{0:T(128)S(1)}, f32[64]{0:T(128)}, u32[]{:S(2)}) copy-start(f32[64]{0:T(128)} %param.15) | copy-start | bytes 772
  0.9 11.0 %copy-start.2 = (bf16[96,256]{1,0:T(8,128)(2,1)S(1)}, bf16[96,256]{1,0:T(8,128)(2,1)}, u32[]{:S(2)}) copy-start(bf16[96,256]{1,0:T(8,128)(2,1)} %constant.314) | copy-start | bytes 147460
  0.9 11.1 %copy-start.7 = (s32[2]{0:T(128)S(1)}, s32[2]{0:T(128)}, u32[]{:S(2)}) copy-start(s32[2]{0:T(128)} %constant.183.clone.1) | copy-start | bytes 28
  2.9 27.1 %copy-start.4 = (s32[1,1,1,2,512]{4,3,2,1,0:T(2,128)S(1)}, s32[1,1,1,2,512]{4,3,2,1,0:T(2,128)}, u32[]{:S(2)}) copy-start(s32[1,1,1,2,512]{4,3,2,1,0:T(2,128)} %param.17) | copy-start | bytes 12292
  2.9 18.9 %all-to-all-start = ((f32[32,20,128]{2,1,0:T(8,128)}), f32[32,20,128]{2,1,0:T(8,128)S(1)}, u32[]{:S(2)}, u32[]{:S(2)}) async-start(f32[32,20,128]{2,1,0:T(8,128)} %copy.72), calls=%async_computation | async-start | bytes 786432 | tf_op jit(solution)/shard_map/all_to_all | solution.py:230
  21.8 0.8 copy-start.1
  25.1 19.6 %copy-start = (f32[128,8,128]{2,1,0:T(8,128)S(1)}, f32[128,8,128]{2,1,0:T(8,128)}, u32[]{:S(2)}) copy-start(f32[128,8,128]{2,1,0:T(8,128)} %shard_map.82.own) | copy-start | bytes 1572868
  26.1 23.3 %copy-start.3 = (bf16[80,96]{1,0:T(8,128)(2,1)S(1)}, bf16[80,96]{1,0:T(8,128)(2,1)}, u32[]{:S(2)}) copy-start(bf16[80,96]{1,0:T(8,128)(2,1)} %constant.212) | copy-start | bytes 46084
  26.1 6.3 %collective-permute-start.1 = (f32[1,4,8,8,128]{4,3,2,1,0:T(8,128)S(1)}, f32[1,4,8,8,128]{4,3,2,1,0:T(8,128)S(1)}, u32[]{:S(2)}, u32[]{:S(2)}) collective-permute-start(f32[1,4,8,8,128]{4,3,2,1,0:T(8,128)S(1)} %bitcast.117), channel_id=1, source_target_pairs={{32,0},{64,32},{96,64},{0,96},{33,1},{65,33},{97,65},{1,97},{34,2}... | collective-permute-start | bytes 393224 | tf_op jit(solution)/shard_map/ppermute | solution.py:220
  29.9 5.6 %collective-permute-start = (f32[1,4,8,8,128]{4,3,2,1,0:T(8,128)S(1)}, f32[1,4,8,8,128]{4,3,2,1,0:T(8,128)S(1)}, u32[]{:S(2)}, u32[]{:S(2)}) collective-permute-start(f32[1,4,8,8,128]{4,3,2,1,0:T(8,128)S(1)} %bitcast.116), channel_id=1, source_target_pairs={{0,32},{32,64},{64,96},{96,0},{1,33},{33,65},{65,97},{97,1},{2,34}... | collective-permute-start | bytes 393224 | tf_op jit(solution)/shard_map/ppermute | solution.py:217
  36.5 8.1 %collective-permute-start.3 = (f32[6,1,8,8,128]{4,3,2,1,0:T(8,128)S(1)}, f32[6,1,8,8,128]{4,3,2,1,0:T(8,128)S(1)}, u32[]{:S(2)}, u32[]{:S(2)}) collective-permute-start(f32[6,1,8,8,128]{4,3,2,1,0:T(8,128)S(1)} %get-tuple-element.42), channel_id=1, source_target_pairs={{8,0},{16,8},{24,16},{0,24},{9,1},{17,9},{25,17},{1,25},{10,2},{18... | collective-permute-start | bytes 589832 | tf_op jit(solution)/shard_map/ppermute | solution.py:220
  38.1 6.5 %collective-permute-start.2 = (f32[6,1,8,8,128]{4,3,2,1,0:T(8,128)S(1)}, f32[6,1,8,8,128]{4,3,2,1,0:T(8,128)S(1)}, u32[]{:S(2)}, u32[]{:S(2)}) collective-permute-start(f32[6,1,8,8,128]{4,3,2,1,0:T(8,128)S(1)} %get-tuple-element.41), channel_id=1, source_target_pairs={{0,8},{8,16},{16,24},{24,0},{1,9},{9,17},{17,25},{25,1},{2,10},{10... | collective-permute-start | bytes 589832 | tf_op jit(solution)/shard_map/ppermute | solution.py:217
  44.7 4.7 %collective-permute-start.5 = (f32[6,6,1,8,128]{4,3,2,1,0:T(8,128)S(1)}, f32[6,6,1,8,128]{4,3,2,1,0:T(8,128)S(1)}, u32[]{:S(2)}, u32[]{:S(2)}) collective-permute-start(f32[6,6,1,8,128]{4,3,2,1,0:T(8,128)S(1)} %get-tuple-element.40), channel_id=1, source_target_pairs={{1,0},{2,1},{3,2},{4,3},{5,4},{6,5},{7,6},{0,7},{9,8},{10,9},{11,1... | collective-permute-start | bytes 442376 | tf_op jit(solution)/shard_map/ppermute | solution.py:220
  46.0 6.1 %collective-permute-start.4 = (f32[6,6,1,8,128]{4,3,2,1,0:T(8,128)S(1)}, f32[6,6,1,8,128]{4,3,2,1,0:T(8,128)S(1)}, u32[]{:S(2)}, u32[]{:S(2)}) collective-permute-start(f32[6,6,1,8,128]{4,3,2,1,0:T(8,128)S(1)} %get-tuple-element.39), channel_id=1, source_target_pairs={{0,1},{1,2},{2,3},{3,4},{4,5},{5,6},{6,7},{7,0},{8,9},{9,10},{10,1... | collective-permute-start | bytes 442376 | tf_op jit(solution)/shard_map/ppermute | solution.py:217

commit v2 on v1

v2 whole, which is shorter than its diff:
```python
import math

import jax
import jax.numpy as jnp
import numpy as np
from jax import lax
from jax.experimental import pallas as pl
from jax.experimental.pallas import tpu as pltpu
from jax.sharding import PartitionSpec as P

F32 = jnp.float32
BF16 = jnp.bfloat16

GRID = 4
LAYERS = 8
CELL = 11.0
LIMIT = 97.0
COULOMB = 332.0636

ROW_X, ROW_Y, ROW_Z, ROW_C, ROW_TYPE, ROW_Q, ROW_ONE, ROW_CC = range(8)
TYPES = 64
ORDER = 13
NX = 32
NY = 48
NZ = TYPES + 32
BATCH = 4
NEAR = 240
SENT = 56


def placements():
    home = np.zeros((32, NX), np.float32)
    src_w = np.zeros((NX, 32), np.float32)
    src_c = np.zeros((NX, 32), np.float32)
    at = 0

    def term(row, part):
        return part * 8 + row

    for row in (ROW_X, ROW_Y, ROW_Z):
        for i, j in ((0, 0), (0, 1), (1, 0), (1, 1), (0, 2), (2, 0)):
            home[term(row, i), at] = 1.0
            src_w[at, term(row, j)] = -2.0
            at += 1
    for part in range(3):
        home[term(ROW_Q, part), at] = 1.0
        src_w[at, term(ROW_ONE, 0)] = 1.0
        at += 1
    for part in range(3):
        home[term(ROW_ONE, 0), at] = 1.0
        src_w[at, term(ROW_Q, part)] = 1.0
        at += 1
    home[term(ROW_ONE, 0), at] = 1.0
    src_w[at, term(ROW_ONE, 0)] = 16.0
    at += 1
    for i, j in ((0, 0), (0, 1), (1, 0), (1, 1), (0, 2), (2, 0)):
        home[term(ROW_CC, i), at] = 1.0
        src_c[at, term(ROW_C, j)] = 1.0
        at += 1
    place_r = np.zeros((16, 32), np.float32)
    for k, row in enumerate((ROW_X, ROW_Y, ROW_Z)):
        for part in range(3):
            place_r[3 * k + part, term(row, part)] = 1.0
    place_r[9, term(ROW_ONE, 0)] = 1.0
    return home, src_w, src_c, place_r


def weights(lj_sigma, lj_epsilon):
    root = jnp.sqrt(lj_epsilon)
    half = 0.5 * lj_sigma
    powers = [jnp.ones_like(half)]
    for _ in range(ORDER - 1):
        powers.append(powers[-1] * half)

    def halves(table):
        high = lax.reduce_precision(table, 8, 7)
        return high, table - high

    h_high, h_low = halves(jnp.stack([root * p for p in powers]))
    zero = jnp.zeros_like(half)
    p12 = jnp.stack([root * powers[12 - k] * (48.0 * math.comb(12, k)) for k in range(ORDER)])
    p6 = jnp.stack(
        [root * powers[6 - k] * (24.0 * math.comb(6, k)) if k <= 6 else zero for k in range(ORDER)]
    )
    pad = jnp.zeros((NY - 3 * ORDER, TYPES), F32)
    home_y = jnp.concatenate([h_high, h_high, h_low, pad])
    src_y = []
    for table in (p12, p6):
        high, low = halves(table)
        src_y += [high, low, high, pad]
    home_x, src_w, src_c, place_r = placements()
    home_x = np.pad(home_x, ((TYPES, 0), (0, 128 - NX)))
    home = jnp.concatenate([home_x, jnp.pad(home_y.T, ((0, NZ - TYPES), (0, 128 - NY)))], 1)
    fixed = jnp.concatenate([jnp.zeros((2 * NX + 16, TYPES)), np.concatenate([src_w, src_c, place_r])], 1)
    lj = jnp.concatenate([jnp.concatenate(src_y), jnp.zeros((2 * NY, 32), F32)], 1)
    source = jnp.concatenate([fixed, lj])
    return home.astype(BF16), source.astype(BF16)


def pack_kernel(half_hi, side, coords, charges, types, out):
    upper = half_hi[0] == 1
    back_y = side[0] == 3
    kinds = types[...].astype(F32)

    def next_y(value):
        ahead = jnp.concatenate([value[8:], value[:8]])
        behind = jnp.concatenate([value[24:], value[:24]])
        return jnp.where(back_y, behind, ahead)

    for q in range(5):
        for cell in range(5):

            def rows(k):
                if q < 3:
                    return coords[q, 32 * k : 32 * k + 32]
                return charges[32 * k : 32 * k + 32] if q == 3 else kinds[32 * k : 32 * k + 32]

            if cell < 4:
                value = rows(cell)
            else:
                ahead = pltpu.roll(rows(0).reshape(4, 8, 128), 7, 1)
                behind = pltpu.roll(rows(3).reshape(4, 8, 128), 1, 1)
                value = jnp.where(upper, behind, ahead).reshape(32, 128)
            out[pl.ds(5 * cell + q, 32, stride=SENT), :] = value
            out[pl.ds(25 + 5 * cell + q, 32, stride=SENT), :] = next_y(value)


def unpack_kernel(arrived, out):
    row = lax.broadcasted_iota(jnp.int32, (8, 128), 0)

    def body(s, carry):
        cell_x, cell_y, upper = s // 8, s // 2 % 4, s % 2
        for c in range(10):
            place_y = cell_y + 1
            if c >= 5:
                place_y = jnp.where(cell_y == 0, GRID + 1, 0)
            place_z = upper * 4 + c % 5 + 1 if c % 5 < 4 else jnp.where(upper == 1, 0, LAYERS + 1)
            place = (cell_x * (GRID + 2) + place_y) * (LAYERS + 2) + place_z
            if c >= 5:
                inner = jnp.logical_and(cell_y > 0, cell_y < GRID - 1)
                place = jnp.where(inner, NEAR, place)
            block = jnp.concatenate([arrived[s, 5 * c : 5 * c + 5], jnp.zeros((3, 128), F32)])
            off_x = cell_x.astype(F32) * CELL - 2 * CELL
            off_y = place_y.astype(F32) * CELL - 3 * CELL
            off_z = place_z.astype(F32) * CELL - 5 * CELL
            off = jnp.where(row == ROW_X, off_x, 0.0) + jnp.where(row == ROW_Y, off_y, 0.0)
            out[place] = block + (off + jnp.where(row == ROW_Z, off_z, 0.0))
        return carry

    lax.fori_loop(0, 32, body, 0, unroll=2)


def powers_of(w):
    u = lax.rsqrt(w)
    inv = u * u
    inv2 = inv * inv
    inv4 = inv2 * inv2
    return inv4 * (inv2 * inv), inv4, u * inv


def factors(block, off_x=None):
    row = lax.broadcasted_iota(jnp.int32, (8, 128), 0)
    kind = lax.broadcasted_iota(jnp.int32, (TYPES, 128), 0)
    moved = block if off_x is None else block + jnp.where(row == ROW_X, off_x, 0.0)
    square = jnp.sum(jnp.where(row < 3, moved * moved, 0.0), axis=0, keepdims=True)
    moved = jnp.where(row == ROW_Q, square, jnp.where(row == ROW_ONE, 1.0, moved))
    moved = jnp.where(row == ROW_CC, COULOMB * block[ROW_C : ROW_C + 1], moved)
    high = moved.astype(BF16).astype(F32)
    rest = moved - high
    mid = rest.astype(BF16).astype(F32)
    hot = jnp.where(block[ROW_TYPE : ROW_TYPE + 1].astype(jnp.int32) == kind, 1.0, 0.0)
    return jnp.concatenate([hot, high, mid, rest - mid, jnp.zeros((8, 128), F32)]).astype(BF16)


def store_source(p, z, w_src, rx, ry, rr):
    made = jnp.dot(w_src[...], z, preferred_element_type=F32).astype(BF16)
    rx[p, :, :128] = made[:NX]
    rx[p, :, 128:] = made[NX : 2 * NX]
    rr[p, :, :128] = made[2 * NX : 2 * NX + 16]
    rr[p, :, 128:] = made[2 * NX : 2 * NX + 16]
    at = 2 * NX + 16
    ry[p, :, :128] = made[at : at + NY]
    ry[p, :, 128:] = made[at + NY :]


def store_home(b, z, w_home, lx, ly):
    made = lax.dot_general(z, w_home[...], (((0,), (0,)), ((), ())), preferred_element_type=F32)
    lx[b] = made[:, :128].astype(BF16)
    ly[b] = made[:, 128:].astype(BF16)


def all_tiles(first, pairs, ids, lx, ly, rx, ry, rr, acc, buf_a, buf_b):
    k7, k4, k3 = powers_of(jnp.full((8, 128), LIMIT, F32))

    def quantities(buf, batch):
        for q in range(BATCH):
            h, j = ids[0, batch * BATCH + q], ids[1, batch * BATCH + q]
            buf[q, 0] = jnp.dot(lx[h][:, :NX], rx[j], preferred_element_type=F32)
            buf[q, 1] = jnp.dot(ly[h][:, :NY], ry[j], preferred_element_type=F32)

    def forces(buf, batch):
        for q in range(BATCH):
            j, h = ids[1, batch * BATCH + q], ids[2, batch * BATCH + q]

            def part(i, side):
                return buf[q, i, :, 128 * side : 128 * side + 128].reshape(16, 8, 128)

            p7, p4, p3 = powers_of(jnp.minimum(part(0, 0), LIMIT))
            push = (p7 - k7) * part(1, 0) - (p4 - k4) * part(1, 1) + (p3 - k3) * part(0, 1)
            push = push.reshape(128, 128)
            high = push.astype(BF16)
            low = (push - high.astype(F32)).astype(BF16)
            acc[h] += lax.dot_general(
                rr[j],
                jnp.concatenate([high, low], 1),
                (((1,), (1,)), ((), ())),
                preferred_element_type=F32,
            )

    @pl.when(pairs > 0)
    def _():
        last = 2 * (first + pairs) - 1
        quantities(buf_a, 2 * first)

        def body(i, carry):
            quantities(buf_b, 2 * i + 1)
            forces(buf_a, 2 * i)
            quantities(buf_a, jnp.minimum(2 * i + 2, last))
            forces(buf_b, 2 * i + 1)
            return carry

        lax.fori_loop(first, first + pairs, body, 0)


def near_place(b):
    return (b // (GRID * LAYERS) * (GRID + 2) + b // LAYERS % GRID + 1) * (LAYERS + 2) + b % LAYERS + 1


def near_kernel(steps, ids, region, w_home, w_src, acc, lx, ly, rx, ry, rr, buf_a, buf_b):
    def owned(b, carry):
        p = near_place(b)
        z = factors(region[p])
        store_source(p, z, w_src, rx, ry, rr)
        store_home(b, z, w_home, lx, ly)
        return carry

    def rim(i, carry):
        side, at = i // 28, i % 28
        place_y = jnp.where(at < 10, 0, jnp.where(at < 20, GRID + 1, 1 + (at - 20) // 2))
        place_z = jnp.where(at < 20, at % 10, (at - 20) % 2 * (LAYERS + 1))
        p = (side * (GRID + 2) + place_y) * (LAYERS + 2) + place_z
        store_source(p, factors(region[p]), w_src, rx, ry, rr)
        return carry

    lax.fori_loop(0, 128, owned, 0, unroll=8)
    lax.fori_loop(0, 112, rim, 0, unroll=8)
    acc[...] = jnp.zeros_like(acc)
    all_tiles(0, steps[0], ids, lx, ly, rx, ry, rr, acc, buf_a, buf_b)


def far_kernel(steps, ids, low, high, region, w_src, lx, ly, acc, out, acc_out, rx, ry, rr, buf_a, buf_b):
    def prepare(p, carry):
        store_source(p, factors(low[p], -44.0), w_src, rx, ry, rr)
        store_source(p + 60, factors(high[p], 44.0), w_src, rx, ry, rr)
        return carry

    lax.fori_loop(0, 60, prepare, 0, unroll=4)
    all_tiles(steps[0], steps[1], ids, lx, ly, rx, ry, rr, acc_out, buf_a, buf_b)
    for x in range(GRID):
        for y in range(GRID):
            b = (x * GRID + y) * LAYERS
            p = (x * (GRID + 2) + y + 1) * (LAYERS + 2) + 1
            total = acc_out[b : b + LAYERS, 9]
            for c in range(3):
                weighed = acc_out[b : b + LAYERS, 3 * c] + acc_out[b : b + LAYERS, 3 * c + 1]
                weighed = weighed + acc_out[b : b + LAYERS, 3 * c + 2]
                out[c, b : b + LAYERS] = region[p : p + LAYERS, c] * total - weighed


def tile_lists(tiles, blocks):
    home, source = tiles[0], tiles[1]
    slot, member = source // blocks, source % blocks
    step_x = slot // 9 - 1
    place_y = member // LAYERS % GRID + (slot // 3 % 3 - 1) * GRID + 1
    place_z = member % LAYERS + (slot % 3 - 1) * LAYERS + 1
    plane = place_y * (LAYERS + 2) + place_z
    side = jnp.where(step_x == 0, member // (GRID * LAYERS), (step_x + 1) // 2)
    listed = home >= 0
    near = listed & (step_x == 0)
    far = listed & (step_x != 0)
    unit = 2 * BATCH
    order = jnp.arange(home.shape[0])
    upto = order[None, :] <= order[:, None]
    near_at = jnp.sum(jnp.where(upto & near[None, :], 1, 0), 1)
    far_at = jnp.sum(jnp.where(upto & far[None, :], 1, 0), 1)
    near_steps = (jnp.sum(near.astype(jnp.int32)) + unit - 1) // unit
    far_steps = (jnp.sum(far.astype(jnp.int32)) + unit - 1) // unit
    at = jnp.where(near, near_at - 1, jnp.where(far, near_steps * unit + far_at - 1, -1))
    code = home * 256 + side * 60 + plane + 1
    slots = jnp.arange(home.shape[0] + 2 * unit)
    found = jnp.sum(jnp.where(slots[:, None] == at[None, :], code[None, :], 0), 1)
    real = found > 0
    code = jnp.maximum(found - 1, 0)
    ids = jnp.stack([code // 256, code % 256, jnp.where(real, code // 256, blocks)])
    return jnp.stack([near_steps, far_steps]), ids


def per_device(coords, charges, atom_types, lj_sigma, lj_epsilon, tile_list):
    blocks, width = coords.shape[2], coords.shape[3]
    peers = lax.axis_size("gy") * lax.axis_size("gz")
    vmem = pl.BlockSpec(memory_space=pltpu.VMEM)
    smem = pl.BlockSpec(memory_space=pltpu.SMEM)
    gz = lax.axis_index("gz")
    small = pltpu.CompilerParams(vmem_limit_bytes=8 << 20)
    outgoing = pl.pallas_call(
        pack_kernel,
        out_shape=jax.ShapeDtypeStruct((peers * SENT, width), F32),
        in_specs=[smem, smem, vmem, vmem, vmem],
        out_specs=vmem,
        compiler_params=small,
    )((gz % 2).reshape(1), (gz // 2).reshape(1), coords[:, 0], charges[0], atom_types[0])
    arrived = lax.all_to_all(
        outgoing.reshape(peers, SENT, width), ("gy", "gz"), split_axis=0, concat_axis=0, tiled=True
    )
    steps, ids = tile_lists(tile_list[0, 0, 0], blocks)
    w_home, w_src = weights(lj_sigma, lj_epsilon)
    region = pl.pallas_call(
        unpack_kernel,
        out_shape=jax.ShapeDtypeStruct((NEAR + 1, 8, width), F32),
        in_specs=[vmem],
        out_specs=vmem,
        compiler_params=small,
    )(arrived)
    count = lax.axis_size("gx")
    forward = [(i, (i + 1) % count) for i in range(count)]
    backward = [(target, source) for source, target in forward]
    low = lax.ppermute(region[180:240], "gx", forward)
    high = lax.ppermute(region[:60], "gx", backward)

    def source_scratch(n):
        return [
            pltpu.VMEM((n, NX, 256), BF16),
            pltpu.VMEM((n, NY, 256), BF16),
            pltpu.VMEM((n, 16, 256), BF16),
            pltpu.VMEM((BATCH, 2, 128, 256), F32),
            pltpu.VMEM((BATCH, 2, 128, 256), F32),
        ]

    acc_shape = jax.ShapeDtypeStruct((blocks + 1, 16, width), F32)
    factor_shape = jax.ShapeDtypeStruct((blocks, 128, 128), BF16)
    acc, lx, ly = pl.pallas_call(
        near_kernel,
        out_shape=[acc_shape, factor_shape, factor_shape],
        in_specs=[smem, smem, vmem, vmem, vmem],
        out_specs=[vmem] * 3,
        scratch_shapes=source_scratch(NEAR),
        compiler_params=pltpu.CompilerParams(vmem_limit_bytes=28 << 20),
        cost_estimate=pl.CostEstimate(flops=10**10, bytes_accessed=10**7, transcendentals=10**6),
    )(steps, ids, region, w_home, w_src)
    totals, _ = pl.pallas_call(
        far_kernel,
        out_shape=[jax.ShapeDtypeStruct((3, blocks, width), F32), acc_shape],
        in_specs=[smem, smem] + [vmem] * 7,
        out_specs=[vmem] * 2,
        scratch_shapes=source_scratch(120),
        input_output_aliases={8: 1},
        compiler_params=pltpu.CompilerParams(vmem_limit_bytes=24 << 20),
    )(steps, ids, low, high, region, w_src, lx, ly, acc)
    sending = totals.reshape(3, peers, 4, width).transpose(1, 0, 2, 3).reshape(peers, 12, width)
    back = lax.all_to_all(sending, ("gy", "gz"), split_axis=0, concat_axis=0, tiled=True)
    return back.reshape(peers, 3, 4, width).transpose(1, 2, 0, 3).reshape(3, 1, blocks, width)


def solution(mesh):
    return jax.shard_map(
        per_device,
        mesh=mesh,
        in_specs=(
            P(None, "gx", ("gy", "gz"), None),
            P("gx", ("gy", "gz"), None),
            P("gx", ("gy", "gz"), None),
            P(),
            P(),
            P("gx", "gy", "gz", None, None),
        ),
        out_specs=P(None, "gx", ("gy", "gz"), None),
        check_vma=False,
    )
```

time: 142 us -> 107 us (0.75)
  Pallas kernels: 75.9 us -> 47.3 us
  blocking collectives: 15.6 us -> 27.9 us
  waiting for transfers between devices: 18.5 us -> 10.9 us
  other arithmetic: 6.47 us -> 1.54 us
  starting transfers between devices: 17.4 us -> 12.6 us
  local copies, waits for them, and re-layouts: 7.28 us -> 4.78 us
    pallas_call x2 -> x4, Pallas kernels: 75.9 us -> 47.3 us  [the longest x1 34.4 us: per_device(): pl.pallas_call(near_kernel, out_shape=[acc_shape, factor_shape, factor_sh...]
    ppermute x6 -> x2, waiting for transfers between devices: 12.3 us -> 0.01 us  [the longest x1 0.01 us: per_device(): high = lax.ppermute(region[:60], 'gx', backward)]
    all_to_all x1, blocking collectives: 15.6 us -> 27.9 us  [per_device(): lax.all_to_all(sending, ('gy', 'gz'), split_axis=0, concat_axis=0, tiled=...]
    ppermute x6 -> x2, starting transfers between devices: 8.68 us -> 3.83 us  [the longest x1 3.83 us: per_device(): high = lax.ppermute(region[:60], 'gx', backward)]
    all_to_all x1, waiting for transfers between devices: 6.22 us -> 10.9 us  [per_device(): lax.all_to_all(outgoing.reshape(peers, SENT, width), ('gy', 'gz'), split_...]
    another operation x7, other arithmetic: 2.67 us -> 0.17 us  [the longest x1 0.08 us: tile_lists(): return (jnp.stack([near_steps, far_steps]), ids)]
    unnamed x17 -> x16, local copies, waits for them, and re-layouts: 0.79 us -> 2.63 us
    scatter x1 -> x0, local copies, waits for them, and re-layouts: 1.71 us -> none  [weights(): home.at[TYPES:, :NX].set(home_x).at[:TYPES, 128:128 + NY].set(home_y.T)]
  transfers between devices with their start and end apart: 7 -> 3, of which waited for: 5 -> 1; matrix products, arithmetic and copies ran while one was open for 5% -> 3% of each run, Pallas kernels for 0% -> 32%
where the time goes in v2:
time: 107 us; the launch traced here: 106 us
  Pallas kernels  47.3 us (44%)
  blocking collectives  27.9 us (26%)
  starting transfers between devices  12.6 us (12%)
  waiting for transfers between devices  10.9 us (10%)
  local copies, waits for them, and re-layouts  4.78 us (4%)
  between operations  1.55 us (1%)
  other arithmetic  1.54 us (1%)
    pallas_call x1, Pallas kernels, per_device(): pl.pallas_call(near_kernel, out_shape=[acc_shape, factor_shape, factor_sh...  34.4 us
    all_to_all x1, blocking collectives, per_device(): lax.all_to_all(sending, ('gy', 'gz'), split_axis=0, concat_axis=0, tiled=...  27.9 us
    all_to_all x1, waiting for transfers between devices, per_device(): lax.all_to_all(outgoing.reshape(peers, SENT, width), ('gy', 'gz'), split_...  10.9 us
    pallas_call x1, Pallas kernels, per_device(): pl.pallas_call(far_kernel, out_shape=[jax.ShapeDtypeStruct((3, blocks, wi...  10.8 us
    all_to_all x1, starting transfers between devices, per_device(): lax.all_to_all(outgoing.reshape(peers, SENT, width), ('gy', 'gz'), split_...  8.74 us
    ppermute x1, starting transfers between devices, per_device(): high = lax.ppermute(region[:60], 'gx', backward)  3.83 us
    unnamed x16, local copies, waits for them, and re-layouts  2.63 us
  transfers between devices with their start and end apart: 3, of which 1 were waited for; matrix products, arithmetic and copies ran while one was open for 3% of the time, Pallas kernels for 32%

profile of v2, /device:TPU:1, one launch (start us, length us, event | category | flops | bytes accessed | tf_op | source)
XLA Modules:
  0.0 106.5 jit_solution(11805242088546070179)
XLA Ops:
  0.0 0.0 copy-start
  0.0 0.9 copy-done
  0.9 0.0 copy-start.1
  0.9 0.8 copy-done.1
  1.8 0.0 copy-start.2
  1.8 0.8 copy-done.2
  2.6 1.1 %shard_map.82 = f32[1792,128]{1,0:T(8,128)} custom-call(s32[1]{0:T(128)} %bitcast.4.half_hi, s32[1]{0:T(128)} %bitcast.5.side, f32[3,128,128]{2,1,0:T(8,128)S(1)} %bitcast.86, f32[128,128]{1,0:T(8,128)S(1)} %bitcast.87, s32[128,128]{1,0:T(8,128)S(1)} %bitcast.88), custom_call_target="tpu_custom_call" | custom-call | tf_op jit(solution)/shard_map/pallas_call | solution.py:315
  3.7 0.0 copy-start.5
  3.7 0.0 copy-start.6
  3.7 0.0 copy-start.7
  3.7 0.0 copy-start.4
  3.7 0.0 copy-start.3
  3.7 8.7 %all-to-all-start = ((f32[32,56,128]{2,1,0:T(8,128)}), f32[32,56,128]{2,1,0:T(8,128)S(1)}, u32[]{:S(2)}, u32[]{:S(2)}) async-start(f32[32,56,128]{2,1,0:T(8,128)} %bitcast.9), calls=%async_computation | async-start | bytes 1835008 | tf_op jit(solution)/shard_map/all_to_all | solution.py:322
  12.4 0.0 copy-done.5
  12.5 0.7 convert_reduce_fusion.1
  14.5 0.2 select_reduce_fusion.1
  14.8 0.2 select_reduce_fusion
  15.0 0.0 copy-done.6
  15.0 0.0 copy-done.7
  15.1 0.1 stack.170
  15.2 0.1 copy.60
  15.4 0.1 stack.156
  15.5 0.1 copy.59
  15.6 0.1 pad.15.clone
  15.7 0.7 concatenate.23
  16.5 0.1 pad_add_fusion.1.steps
  16.5 0.0 copy-done.4
  16.6 0.1 maximum_bitcast_fusion
  16.7 0.0 copy-done.3
  16.7 10.9 %all-to-all-done.arrived = f32[32,56,128]{2,1,0:T(8,128)S(1)} async-done(((f32[32,56,128]{2,1,0:T(8,128)}), f32[32,56,128]{2,1,0:T(8,128)S(1)}, u32[]{:S(2)}, u32[]{:S(2)}) %all-to-all-start) | async-done | bytes 917536 | tf_op jit(solution)/shard_map/all_to_all | solution.py:322
  27.6 1.0 shard_map.83.region
  28.7 3.8 %collective-permute-start.1 = (f32[60,8,128]{2,1,0:T(8,128)S(1)}, f32[60,8,128]{2,1,0:T(8,128)S(1)}, u32[]{:S(2)}, u32[]{:S(2)}) collective-permute-start(f32[60,8,128]{2,1,0:T(8,128)S(1)} %get-tuple-element.31), channel_id=1, source_target_pairs={{32,0},{64,32},{96,64},{0,96},{33,1},{65,33},{97,65},{1,97},{34,2}... | collective-permute-start | bytes 737288 | tf_op jit(solution)/shard_map/ppermute | solution.py:338
  32.5 0.0 collective-permute-start
  32.5 34.4 %shard_map.84 = (f32[129,16,128]{2,1,0:T(8,128)S(1)}, bf16[128,128,128]{2,1,0:T(8,128)(2,1)S(1)}, bf16[128,128,128]{2,1,0:T(8,128)(2,1)S(1)}) custom-call(s32[2]{0:T(128)S(1)} %pad_add_fusion.1.steps, s32[3,528]{1,0:T(4,128)S(1)} %pad_add_fusion.ids, f32[241,8,128]{2,1,0:T(8,128)S(1)} %shard_map.83.region, bf16[96,256]{1,0:T(8,128)(2,1)S(1)} %fusion.4.w_home, ...), custom_call_target="tpu_custom_call" | custom-call | flops 10000000000 | bytes 10000000 | tf_op jit(solution)/shard_map/pallas_call | solution.py:351
  66.9 0.0 collective-permute-done.1.high
  66.9 0.0 collective-permute-done.low
  66.9 10.8 %shard_map.85 = (f32[3,128,128]{2,1,0:T(8,128)S(1)}, f32[129,16,128]{2,1,0:T(8,128)S(1)}) custom-call(s32[2]{0:T(128)S(1)} %pad_add_fusion.1.steps, s32[3,528]{1,0:T(4,128)S(1)} %pad_add_fusion.ids, f32[60,8,128]{2,1,0:T(8,128)S(1)} %collective-permute-done.low, f32[60,8,128]{2,1,0:T(8,128)S(1)} %collective-permute-done.1.high, ...), custom_call_target="tpu_custom_call", output_to_operand_aliasing={{1}: (8, {})} | custom-call | tf_op jit(solution)/shard_map/pallas_call | solution.py:360
  77.8 0.1 copy.64
  77.9 27.9 %all_to_all.10 = f32[32,12,128]{2,1,0:T(8,128)S(1)} all-to-all(f32[32,12,128]{2,1,0:T(8,128)S(1)} %copy.64), channel_id=1, replica_groups=mesh['gx'=4,'gy'=4,'gz'=8] {'gy','gz'}, dimensions={0} | all-to-all | bytes 393216 | tf_op jit(solution)/shard_map/all_to_all | solution.py:370
  105.7 0.7 copy.65
  (25 shorter events, 0.3 us)
Async XLA Ops:
  0.0 0.9 copy-start
  0.9 0.8 copy-start.1
  1.8 0.8 copy-start.2
  3.7 8.8 %copy-start.5 = (s32[1,1,1,2,512]{4,3,2,1,0:T(2,128)S(1)}, s32[1,1,1,2,512]{4,3,2,1,0:T(2,128)}, u32[]{:S(2)}) copy-start(s32[1,1,1,2,512]{4,3,2,1,0:T(2,128)} %param.13) | copy-start | bytes 12292
  3.7 11.3 %copy-start.6 = (f32[64]{0:T(128)S(1)}, f32[64]{0:T(128)}, u32[]{:S(2)}) copy-start(f32[64]{0:T(128)} %param.11) | copy-start | bytes 772
  3.7 11.4 %copy-start.7 = (f32[64]{0:T(128)S(1)}, f32[64]{0:T(128)}, u32[]{:S(2)}) copy-start(f32[64]{0:T(128)} %param.12) | copy-start | bytes 772
  3.7 12.9 %copy-start.4 = (bf16[80,96]{1,0:T(8,128)(2,1)S(1)}, bf16[80,96]{1,0:T(8,128)(2,1)}, u32[]{:S(2)}) copy-start(bf16[80,96]{1,0:T(8,128)(2,1)} %constant.240) | copy-start | bytes 46084
  3.7 13.0 %copy-start.3 = (bf16[96,128]{1,0:T(8,128)(2,1)S(1)}, bf16[96,128]{1,0:T(8,128)(2,1)}, u32[]{:S(2)}) copy-start(bf16[96,128]{1,0:T(8,128)(2,1)} %constant.241) | copy-start | bytes 73732
  3.7 23.9 %all-to-all-start = ((f32[32,56,128]{2,1,0:T(8,128)}), f32[32,56,128]{2,1,0:T(8,128)S(1)}, u32[]{:S(2)}, u32[]{:S(2)}) async-start(f32[32,56,128]{2,1,0:T(8,128)} %bitcast.9), calls=%async_computation | async-start | bytes 1835008 | tf_op jit(solution)/shard_map/all_to_all | solution.py:322
  28.7 38.2 %collective-permute-start.1 = (f32[60,8,128]{2,1,0:T(8,128)S(1)}, f32[60,8,128]{2,1,0:T(8,128)S(1)}, u32[]{:S(2)}, u32[]{:S(2)}) collective-permute-start(f32[60,8,128]{2,1,0:T(8,128)S(1)} %get-tuple-element.31), channel_id=1, source_target_pairs={{32,0},{64,32},{96,64},{0,96},{33,1},{65,33},{97,65},{1,97},{34,2}... | collective-permute-start | bytes 737288 | tf_op jit(solution)/shard_map/ppermute | solution.py:338
  32.5 34.4 %collective-permute-start = (f32[60,8,128]{2,1,0:T(8,128)S(1)}, f32[60,8,128]{2,1,0:T(8,128)S(1)}, u32[]{:S(2)}, u32[]{:S(2)}) collective-permute-start(f32[60,8,128]{2,1,0:T(8,128)S(1)} %get-tuple-element.32), channel_id=1, source_target_pairs={{0,32},{32,64},{64,96},{96,0},{1,33},{33,65},{65,97},{97,1},{2,34}... | collective-permute-start | bytes 737288 | tf_op jit(solution)/shard_map/ppermute | solution.py:337

commit v3 on v2

--- a/solution.py
+++ b/solution.py
@@ -24,6 +24,8 @@
 NY = 48
 NZ = TYPES + 32
 BATCH = 4
+GROUP = 8
+FAR_GROUP = 10
 NEAR = 240
 SENT = 56
 
@@ -97,7 +99,17 @@
     return home.astype(BF16), source.astype(BF16)
 
 
-def pack_kernel(half_hi, side, coords, charges, types, out):
+def pack_kernel(half_hi, side, coords_in, charges_in, types_in, out, coords, charges, types, sems):
+    copies = [
+        pltpu.make_async_copy(source, target, sems.at[i])
+        for i, (source, target) in enumerate(
+            ((coords_in, coords), (charges_in, charges), (types_in, types))
+        )
+    ]
+    for copy in copies:
+        copy.start()
+    for copy in copies:
+        copy.wait()
     upper = half_hi[0] == 1
     back_y = side[0] == 3
     kinds = types[...].astype(F32)
@@ -172,21 +184,26 @@
     return jnp.concatenate([hot, high, mid, rest - mid, jnp.zeros((8, 128), F32)]).astype(BF16)
 
 
-def store_source(p, z, w_src, rx, ry, rr):
+def store_source(places, z, w_src, rx, ry, rr):
     made = jnp.dot(w_src[...], z, preferred_element_type=F32).astype(BF16)
-    rx[p, :, :128] = made[:NX]
-    rx[p, :, 128:] = made[NX : 2 * NX]
-    rr[p, :, :128] = made[2 * NX : 2 * NX + 16]
-    rr[p, :, 128:] = made[2 * NX : 2 * NX + 16]
-    at = 2 * NX + 16
-    ry[p, :, :128] = made[at : at + NY]
-    ry[p, :, 128:] = made[at + NY :]
-
-
-def store_home(b, z, w_home, lx, ly):
+    for g, p in enumerate(places):
+        own = made[:, 128 * g : 128 * g + 128]
+        rx[p, :, :128] = own[:NX]
+        rx[p, :, 128:] = own[NX : 2 * NX]
+        rr[p, :, :128] = own[2 * NX : 2 * NX + 16]
+        rr[p, :, 128:] = own[2 * NX : 2 * NX + 16]
+        at = 2 * NX + 16
+        ry[p, :, :128] = own[at : at + NY]
+        ry[p, :, 128:] = own[at + NY :]
+
+
+def store_home(first, z, w_home, lx, ly):
     made = lax.dot_general(z, w_home[...], (((0,), (0,)), ((), ())), preferred_element_type=F32)
-    lx[b] = made[:, :128].astype(BF16)
-    ly[b] = made[:, 128:].astype(BF16)
+    made = made.astype(BF16)
+    for g in range(GROUP):
+        own = made[128 * g : 128 * g + 128]
+        lx[first + g] = own[:, :128]
+        ly[first + g] = own[:, 128:]
 
 
 def all_tiles(first, pairs, ids, lx, ly, rx, ry, rr, acc, buf_a, buf_b):
@@ -237,34 +254,41 @@
 
 
 def near_kernel(steps, ids, region, w_home, w_src, acc, lx, ly, rx, ry, rr, buf_a, buf_b):
-    def owned(b, carry):
-        p = near_place(b)
-        z = factors(region[p])
-        store_source(p, z, w_src, rx, ry, rr)
-        store_home(b, z, w_home, lx, ly)
+    def owned(i, carry):
+        first = near_place(i * GROUP)
+        places = [first + g for g in range(GROUP)]
+        z = jnp.concatenate([factors(region[p]) for p in places], 1)
+        store_source(places, z, w_src, rx, ry, rr)
+        store_home(i * GROUP, z, w_home, lx, ly)
         return carry
 
-    def rim(i, carry):
+    def rim_place(i):
         side, at = i // 28, i % 28
         place_y = jnp.where(at < 10, 0, jnp.where(at < 20, GRID + 1, 1 + (at - 20) // 2))
         place_z = jnp.where(at < 20, at % 10, (at - 20) % 2 * (LAYERS + 1))
-        p = (side * (GRID + 2) + place_y) * (LAYERS + 2) + place_z
-        store_source(p, factors(region[p]), w_src, rx, ry, rr)
+        return (side * (GRID + 2) + place_y) * (LAYERS + 2) + place_z
+
+    def rim(i, carry):
+        places = [rim_place(i * GROUP + g) for g in range(GROUP)]
+        z = jnp.concatenate([factors(region[p]) for p in places], 1)
+        store_source(places, z, w_src, rx, ry, rr)
         return carry
 
-    lax.fori_loop(0, 128, owned, 0, unroll=8)
-    lax.fori_loop(0, 112, rim, 0, unroll=8)
+    lax.fori_loop(0, 128 // GROUP, owned, 0, unroll=4)
+    lax.fori_loop(0, 112 // GROUP, rim, 0, unroll=7)
     acc[...] = jnp.zeros_like(acc)
     all_tiles(0, steps[0], ids, lx, ly, rx, ry, rr, acc, buf_a, buf_b)
 
 
 def far_kernel(steps, ids, low, high, region, w_src, lx, ly, acc, out, acc_out, rx, ry, rr, buf_a, buf_b):
-    def prepare(p, carry):
-        store_source(p, factors(low[p], -44.0), w_src, rx, ry, rr)
-        store_source(p + 60, factors(high[p], 44.0), w_src, rx, ry, rr)
+    def prepare(i, carry):
+        for k, (plane, off_x) in enumerate(((low, -44.0), (high, 44.0))):
+            places = [i * FAR_GROUP + g for g in range(FAR_GROUP)]
+            z = jnp.concatenate([factors(plane[p], off_x) for p in places], 1)
+            store_source([p + 60 * k for p in places], z, w_src, rx, ry, rr)
         return carry
 
-    lax.fori_loop(0, 60, prepare, 0, unroll=4)
+    lax.fori_loop(0, 60 // FAR_GROUP, prepare, 0, unroll=2)
     all_tiles(steps[0], steps[1], ids, lx, ly, rx, ry, rr, acc_out, buf_a, buf_b)
     for x in range(GRID):
         for y in range(GRID):
@@ -315,9 +339,15 @@
     outgoing = pl.pallas_call(
         pack_kernel,
         out_shape=jax.ShapeDtypeStruct((peers * SENT, width), F32),
-        in_specs=[smem, smem, vmem, vmem, vmem],
+        in_specs=[smem, smem] + [pl.BlockSpec(memory_space=pl.ANY)] * 3,
         out_specs=vmem,
-        compiler_params=small,
+        scratch_shapes=[
+            pltpu.VMEM((3, blocks, width), F32),
+            pltpu.VMEM((blocks, width), F32),
+            pltpu.VMEM((blocks, width), jnp.int32),
+            pltpu.SemaphoreType.DMA((3,)),
+        ],
+        compiler_params=pltpu.CompilerParams(vmem_limit_bytes=65011712),
     )((gz % 2).reshape(1), (gz // 2).reshape(1), coords[:, 0], charges[0], atom_types[0])
     arrived = lax.all_to_all(
         outgoing.reshape(peers, SENT, width), ("gy", "gz"), split_axis=0, concat_axis=0, tiled=True

time: 107 us -> 95.3 us (0.89); the launches traced: 106 us -> 96.3 us
  blocking collectives: 27.9 us -> 13.9 us
  Pallas kernels: 47.3 us -> 53.7 us
  local copies, waits for them, and re-layouts: 4.78 us -> 2.18 us
    all_to_all x1, blocking collectives: 27.9 us -> 13.9 us  [per_device(): lax.all_to_all(sending, ('gy', 'gz'), split_axis=0, concat_axis=0, tiled=...]
    pallas_call x1, Pallas kernels: 34.4 us -> 39.9 us  [per_device(): pl.pallas_call(near_kernel, out_shape=[acc_shape, factor_shape, factor_sh...]
    unnamed x16 -> x10, local copies, waits for them, and re-layouts: 2.63 us -> 0.03 us
  transfers between devices with their start and end apart: 3 -> 3, of which waited for: 1 -> 1; matrix products, arithmetic and copies ran while one was open for 3% -> 3% of each run, Pallas kernels for 32% -> 41%
where the time goes in v3:
time: 95.3 us; the launch traced here: 96.3 us
  Pallas kernels  53.7 us (56%)
  blocking collectives  13.9 us (15%)
  starting transfers between devices  12.6 us (13%)
  waiting for transfers between devices  10.8 us (11%)
  local copies, waits for them, and re-layouts  2.18 us (2%)
  between operations  1.64 us (2%)
  other arithmetic  1.56 us (2%)
    pallas_call x1, Pallas kernels, per_device(): pl.pallas_call(near_kernel, out_shape=[acc_shape, factor_shape, factor_sh...  39.9 us
    all_to_all x1, blocking collectives, per_device(): lax.all_to_all(sending, ('gy', 'gz'), split_axis=0, concat_axis=0, tiled=...  13.9 us
    all_to_all x1, waiting for transfers between devices, per_device(): lax.all_to_all(outgoing.reshape(peers, SENT, width), ('gy', 'gz'), split_...  10.8 us
    pallas_call x1, Pallas kernels, per_device(): pl.pallas_call(far_kernel, out_shape=[jax.ShapeDtypeStruct((3, blocks, wi...  10.7 us
    all_to_all x1, starting transfers between devices, per_device(): lax.all_to_all(outgoing.reshape(peers, SENT, width), ('gy', 'gz'), split_...  8.74 us
    ppermute x1, starting transfers between devices, per_device(): high = lax.ppermute(region[:60], 'gx', backward)  3.83 us
    pallas_call x1, Pallas kernels, per_device(): pl.pallas_call(pack_kernel, out_shape=jax.ShapeDtypeStruct((peers * SENT,...  2.07 us
  transfers between devices with their start and end apart: 3, of which 1 were waited for; matrix products, arithmetic and copies ran while one was open for 3% of the time, Pallas kernels for 41%

profile of v3, /device:TPU:1, one launch (start us, length us, event | category | flops | bytes accessed | tf_op | source)
XLA Modules:
  0.0 96.3 jit_solution(13214881604405355177)
XLA Ops:
  0.0 2.1 %shard_map.82 = f32[1792,128]{1,0:T(8,128)} custom-call(s32[1]{0:T(128)} %bitcast.4.half_hi, s32[1]{0:T(128)} %bitcast.5.side, f32[3,128,128]{2,1,0:T(8,128)} %bitcast.88, f32[128,128]{1,0:T(8,128)} %bitcast.89, s32[128,128]{1,0:T(8,128)} %bitcast.90), custom_call_target="tpu_custom_call" | custom-call | tf_op jit(solution)/shard_map/pallas_call | solution.py:339
  2.1 0.0 copy-start.2
  2.1 0.0 copy-start.3
  2.1 0.0 copy-start.4
  2.1 0.0 copy-start.1
  2.1 0.0 copy-start
  2.1 8.7 %all-to-all-start = ((f32[32,56,128]{2,1,0:T(8,128)}), f32[32,56,128]{2,1,0:T(8,128)S(1)}, u32[]{:S(2)}, u32[]{:S(2)}) async-start(f32[32,56,128]{2,1,0:T(8,128)} %bitcast.86), calls=%async_computation | async-start | bytes 1835008 | tf_op jit(solution)/shard_map/all_to_all | solution.py:352
  10.9 0.0 copy-done.2
  11.0 0.7 convert_reduce_fusion.1
  13.1 0.2 select_reduce_fusion.1
  13.3 0.2 select_reduce_fusion
  13.5 0.0 copy-done.3
  13.5 0.0 copy-done.4
  13.6 0.1 stack.170
  13.7 0.1 copy.60
  13.9 0.1 stack.156
  14.0 0.1 copy.59
  14.1 0.1 pad.15.clone
  14.2 0.7 concatenate.23
  15.0 0.1 pad_add_fusion.1.steps
  15.1 0.0 copy-done.1
  15.1 0.1 maximum_bitcast_fusion
  15.2 0.0 copy-done
  15.2 10.8 %all-to-all-done.arrived = f32[32,56,128]{2,1,0:T(8,128)S(1)} async-done(((f32[32,56,128]{2,1,0:T(8,128)}), f32[32,56,128]{2,1,0:T(8,128)S(1)}, u32[]{:S(2)}, u32[]{:S(2)}) %all-to-all-start) | async-done | bytes 917536 | tf_op jit(solution)/shard_map/all_to_all | solution.py:352
  26.0 1.0 %shard_map.83.region = f32[241,8,128]{2,1,0:T(8,128)S(1)} custom-call(f32[32,56,128]{2,1,0:T(8,128)S(1)} %all-to-all-done.arrived), custom_call_target="tpu_custom_call" | custom-call | tf_op jit(solution)/shard_map/pallas_call | solution.py:357
  27.1 3.8 %collective-permute-start.1 = (f32[60,8,128]{2,1,0:T(8,128)S(1)}, f32[60,8,128]{2,1,0:T(8,128)S(1)}, u32[]{:S(2)}, u32[]{:S(2)}) collective-permute-start(f32[60,8,128]{2,1,0:T(8,128)S(1)} %get-tuple-element.31), channel_id=1, source_target_pairs={{32,0},{64,32},{96,64},{0,96},{33,1},{65,33},{97,65},{1,97},{34,2}... | collective-permute-start | bytes 737288 | tf_op jit(solution)/shard_map/ppermute | solution.py:368
  30.9 0.0 collective-permute-start
  30.9 39.9 %shard_map.84 = (f32[129,16,128]{2,1,0:T(8,128)S(1)}, bf16[128,128,128]{2,1,0:T(8,128)(2,1)S(1)}, bf16[128,128,128]{2,1,0:T(8,128)(2,1)S(1)}) custom-call(s32[2]{0:T(128)S(1)} %pad_add_fusion.1.steps, s32[3,528]{1,0:T(4,128)S(1)} %pad_add_fusion.ids, f32[241,8,128]{2,1,0:T(8,128)S(1)} %shard_map.83.region, bf16[96,256]{1,0:T(8,128)(2,1)S(1)} %fusion.4.w_home, ...), custom_call_target="tpu_custom_call" | custom-call | flops 10000000000 | bytes 10000000 | tf_op jit(solution)/shard_map/pallas_call | solution.py:381
  70.8 0.0 collective-permute-done.1.high
  70.8 0.0 collective-permute-done.low
  70.8 10.7 %shard_map.85 = (f32[3,128,128]{2,1,0:T(8,128)S(1)}, f32[129,16,128]{2,1,0:T(8,128)S(1)}) custom-call(s32[2]{0:T(128)S(1)} %pad_add_fusion.1.steps, s32[3,528]{1,0:T(4,128)S(1)} %pad_add_fusion.ids, f32[60,8,128]{2,1,0:T(8,128)S(1)} %collective-permute-done.low, f32[60,8,128]{2,1,0:T(8,128)S(1)} %collective-permute-done.1.high, ...), custom_call_target="tpu_custom_call", output_to_operand_aliasing={{1}: (8, {})} | custom-call | tf_op jit(solution)/shard_map/pallas_call | solution.py:390
  81.6 0.1 copy.64
  81.7 13.9 %all_to_all.10 = f32[32,12,128]{2,1,0:T(8,128)S(1)} all-to-all(f32[32,12,128]{2,1,0:T(8,128)S(1)} %copy.64), channel_id=1, replica_groups=mesh['gx'=4,'gy'=4,'gz'=8] {'gy','gz'}, dimensions={0} | all-to-all | bytes 393216 | tf_op jit(solution)/shard_map/all_to_all | solution.py:400
  95.6 0.7 copy.65
  (25 shorter events, 0.3 us)
Async XLA Ops:
  2.1 8.8 %copy-start.2 = (s32[1,1,1,2,512]{4,3,2,1,0:T(2,128)S(1)}, s32[1,1,1,2,512]{4,3,2,1,0:T(2,128)}, u32[]{:S(2)}) copy-start(s32[1,1,1,2,512]{4,3,2,1,0:T(2,128)} %param.13) | copy-start | bytes 12292
  2.1 11.4 %copy-start.3 = (f32[64]{0:T(128)S(1)}, f32[64]{0:T(128)}, u32[]{:S(2)}) copy-start(f32[64]{0:T(128)} %param.11) | copy-start | bytes 772
  2.1 11.4 %copy-start.4 = (f32[64]{0:T(128)S(1)}, f32[64]{0:T(128)}, u32[]{:S(2)}) copy-start(f32[64]{0:T(128)} %param.12) | copy-start | bytes 772
  2.1 12.9 %copy-start.1 = (bf16[80,96]{1,0:T(8,128)(2,1)S(1)}, bf16[80,96]{1,0:T(8,128)(2,1)}, u32[]{:S(2)}) copy-start(bf16[80,96]{1,0:T(8,128)(2,1)} %constant.240) | copy-start | bytes 46084
  2.1 13.1 %copy-start = (bf16[96,128]{1,0:T(8,128)(2,1)S(1)}, bf16[96,128]{1,0:T(8,128)(2,1)}, u32[]{:S(2)}) copy-start(bf16[96,128]{1,0:T(8,128)(2,1)} %constant.241) | copy-start | bytes 73732
  2.1 23.9 %all-to-all-start = ((f32[32,56,128]{2,1,0:T(8,128)}), f32[32,56,128]{2,1,0:T(8,128)S(1)}, u32[]{:S(2)}, u32[]{:S(2)}) async-start(f32[32,56,128]{2,1,0:T(8,128)} %bitcast.86), calls=%async_computation | async-start | bytes 1835008 | tf_op jit(solution)/shard_map/all_to_all | solution.py:352
  27.1 43.7 %collective-permute-start.1 = (f32[60,8,128]{2,1,0:T(8,128)S(1)}, f32[60,8,128]{2,1,0:T(8,128)S(1)}, u32[]{:S(2)}, u32[]{:S(2)}) collective-permute-start(f32[60,8,128]{2,1,0:T(8,128)S(1)} %get-tuple-element.31), channel_id=1, source_target_pairs={{32,0},{64,32},{96,64},{0,96},{33,1},{65,33},{97,65},{1,97},{34,2}... | collective-permute-start | bytes 737288 | tf_op jit(solution)/shard_map/ppermute | solution.py:368
  30.9 39.9 %collective-permute-start = (f32[60,8,128]{2,1,0:T(8,128)S(1)}, f32[60,8,128]{2,1,0:T(8,128)S(1)}, u32[]{:S(2)}, u32[]{:S(2)}) collective-permute-start(f32[60,8,128]{2,1,0:T(8,128)S(1)} %get-tuple-element.32), channel_id=1, source_target_pairs={{0,32},{32,64},{64,96},{96,0},{1,33},{33,65},{65,97},{97,1},{2,34}... | collective-permute-start | bytes 737288 | tf_op jit(solution)/shard_map/ppermute | solution.py:367

commit v4 on v3

--- a/solution.py
+++ b/solution.py
@@ -62,8 +62,8 @@
     place_r = np.zeros((16, 32), np.float32)
     for k, row in enumerate((ROW_X, ROW_Y, ROW_Z)):
         for part in range(3):
-            place_r[3 * k + part, term(row, part)] = 1.0
-    place_r[9, term(ROW_ONE, 0)] = 1.0
+            place_r[4 * part + k, term(row, part)] = 1.0
+    place_r[3, term(ROW_ONE, 0)] = 1.0
     return home, src_w, src_c, place_r
 
 
@@ -209,41 +209,43 @@
 def all_tiles(first, pairs, ids, lx, ly, rx, ry, rr, acc, buf_a, buf_b):
     k7, k4, k3 = powers_of(jnp.full((8, 128), LIMIT, F32))
 
-    def quantities(buf, batch):
+    def quantities(buf, batch, q):
+        h, j = ids[0, batch * BATCH + q], ids[1, batch * BATCH + q]
+        buf[q, 0] = jnp.dot(lx[h][:, :NX], rx[j], preferred_element_type=F32)
+        buf[q, 1] = jnp.dot(ly[h][:, :NY], ry[j], preferred_element_type=F32)
+
+    def forces(buf, batch, q):
+        j, h = ids[1, batch * BATCH + q], ids[2, batch * BATCH + q]
+
+        def part(i, side):
+            return buf[q, i, :, 128 * side : 128 * side + 128].reshape(16, 8, 128)
+
+        p7, p4, p3 = powers_of(jnp.minimum(part(0, 0), LIMIT))
+        push = (p7 - k7) * part(1, 0) - (p4 - k4) * part(1, 1) + (p3 - k3) * part(0, 1)
+        push = push.reshape(128, 128)
+        high = push.astype(BF16)
+        low = (push - high.astype(F32)).astype(BF16)
+        acc[h] += lax.dot_general(
+            rr[j],
+            jnp.concatenate([high, low], 1),
+            (((1,), (1,)), ((), ())),
+            preferred_element_type=F32,
+        )
+
+    def both(buf_next, buf_now, batch_next, batch_now):
         for q in range(BATCH):
-            h, j = ids[0, batch * BATCH + q], ids[1, batch * BATCH + q]
-            buf[q, 0] = jnp.dot(lx[h][:, :NX], rx[j], preferred_element_type=F32)
-            buf[q, 1] = jnp.dot(ly[h][:, :NY], ry[j], preferred_element_type=F32)
-
-    def forces(buf, batch):
-        for q in range(BATCH):
-            j, h = ids[1, batch * BATCH + q], ids[2, batch * BATCH + q]
-
-            def part(i, side):
-                return buf[q, i, :, 128 * side : 128 * side + 128].reshape(16, 8, 128)
-
-            p7, p4, p3 = powers_of(jnp.minimum(part(0, 0), LIMIT))
-            push = (p7 - k7) * part(1, 0) - (p4 - k4) * part(1, 1) + (p3 - k3) * part(0, 1)
-            push = push.reshape(128, 128)
-            high = push.astype(BF16)
-            low = (push - high.astype(F32)).astype(BF16)
-            acc[h] += lax.dot_general(
-                rr[j],
-                jnp.concatenate([high, low], 1),
-                (((1,), (1,)), ((), ())),
-                preferred_element_type=F32,
-            )
+            quantities(buf_next, batch_next, q)
+            forces(buf_now, batch_now, q)
 
     @pl.when(pairs > 0)
     def _():
         last = 2 * (first + pairs) - 1
-        quantities(buf_a, 2 * first)
+        for q in range(BATCH):
+            quantities(buf_a, 2 * first, q)
 
         def body(i, carry):
-            quantities(buf_b, 2 * i + 1)
-            forces(buf_a, 2 * i)
-            quantities(buf_a, jnp.minimum(2 * i + 2, last))
-            forces(buf_b, 2 * i + 1)
+            both(buf_b, buf_a, 2 * i + 1, 2 * i)
+            both(buf_a, buf_b, jnp.minimum(2 * i + 2, last), 2 * i + 1)
             return carry
 
         lax.fori_loop(first, first + pairs, body, 0)
@@ -290,15 +292,17 @@
 
     lax.fori_loop(0, 60 // FAR_GROUP, prepare, 0, unroll=2)
     all_tiles(steps[0], steps[1], ids, lx, ly, rx, ry, rr, acc_out, buf_a, buf_b)
-    for x in range(GRID):
-        for y in range(GRID):
-            b = (x * GRID + y) * LAYERS
-            p = (x * (GRID + 2) + y + 1) * (LAYERS + 2) + 1
-            total = acc_out[b : b + LAYERS, 9]
-            for c in range(3):
-                weighed = acc_out[b : b + LAYERS, 3 * c] + acc_out[b : b + LAYERS, 3 * c + 1]
-                weighed = weighed + acc_out[b : b + LAYERS, 3 * c + 2]
-                out[c, b : b + LAYERS] = region[p : p + LAYERS, c] * total - weighed
+
+    def finish(s, carry):
+        first = near_place(4 * s)
+        for k in range(4):
+            sums = acc_out[4 * s + k]
+            head, tail = sums[:8], sums[8:]
+            weighed = head + pltpu.roll(head, 4, 0) + tail
+            out[s, 3 * k : 3 * k + 3] = (region[first + k] * head[3:4] - weighed)[:3]
+        return carry
+
+    lax.fori_loop(0, 32, finish, 0, unroll=4)
 
 
 def tile_lists(tiles, blocks):
@@ -389,16 +393,15 @@
     )(steps, ids, region, w_home, w_src)
     totals, _ = pl.pallas_call(
         far_kernel,
-        out_shape=[jax.ShapeDtypeStruct((3, blocks, width), F32), acc_shape],
+        out_shape=[jax.ShapeDtypeStruct((peers, 12, width), F32), acc_shape],
         in_specs=[smem, smem] + [vmem] * 7,
         out_specs=[vmem] * 2,
         scratch_shapes=source_scratch(120),
         input_output_aliases={8: 1},
         compiler_params=pltpu.CompilerParams(vmem_limit_bytes=24 << 20),
     )(steps, ids, low, high, region, w_src, lx, ly, acc)
-    sending = totals.reshape(3, peers, 4, width).transpose(1, 0, 2, 3).reshape(peers, 12, width)
-    back = lax.all_to_all(sending, ("gy", "gz"), split_axis=0, concat_axis=0, tiled=True)
-    return back.reshape(peers, 3, 4, width).transpose(1, 2, 0, 3).reshape(3, 1, blocks, width)
+    back = lax.all_to_all(totals, ("gy", "gz"), split_axis=0, concat_axis=0, tiled=True)
+    return back.reshape(peers, 4, 3, width).transpose(2, 1, 0, 3).reshape(3, 1, blocks, width)
 
 
 def solution(mesh):

time: 95.3 us -> 89.2 us (0.936)
  Pallas kernels: 53.7 us -> 38.8 us
  blocking collectives: 13.9 us -> 22.4 us
    pallas_call x1, Pallas kernels: 39.9 us -> 28.2 us  [per_device(): pl.pallas_call(near_kernel, out_shape=[acc_shape, factor_shape, factor_sh...]
    all_to_all x1, blocking collectives: 13.9 us -> 22.4 us  [per_device(): lax.all_to_all(totals, ('gy', 'gz'), split_axis=0, concat_axis=0, tiled=T...]
    pallas_call x1, Pallas kernels: 10.7 us -> 7.5 us  [per_device(): pl.pallas_call(far_kernel, out_shape=[jax.ShapeDtypeStruct((peers, 12, wi...]
  transfers between devices with their start and end apart: 3 -> 3, of which waited for: 1 -> 1; matrix products, arithmetic and copies ran while one was open for 3% -> 3% of each run, Pallas kernels for 41% -> 31%
where the time goes in v4:
time: 89.2 us; the launch traced here: 89.8 us
  Pallas kernels  38.8 us (43%)
  blocking collectives  22.4 us (25%)
  starting transfers between devices  12.6 us (14%)
  waiting for transfers between devices  10.8 us (12%)
  local copies, waits for them, and re-layouts  2.07 us (2%)
  between operations  1.64 us (2%)
  other arithmetic  1.56 us (2%)
    pallas_call x1, Pallas kernels, per_device(): pl.pallas_call(near_kernel, out_shape=[acc_shape, factor_shape, factor_sh...  28.2 us
    all_to_all x1, blocking collectives, per_device(): lax.all_to_all(totals, ('gy', 'gz'), split_axis=0, concat_axis=0, tiled=T...  22.4 us
    all_to_all x1, waiting for transfers between devices, per_device(): lax.all_to_all(outgoing.reshape(peers, SENT, width), ('gy', 'gz'), split_...  10.8 us
    all_to_all x1, starting transfers between devices, per_device(): lax.all_to_all(outgoing.reshape(peers, SENT, width), ('gy', 'gz'), split_...  8.74 us
    pallas_call x1, Pallas kernels, per_device(): pl.pallas_call(far_kernel, out_shape=[jax.ShapeDtypeStruct((peers, 12, wi...  7.5 us
    ppermute x1, starting transfers between devices, per_device(): high = lax.ppermute(region[:60], 'gx', backward)  3.83 us
    pallas_call x1, Pallas kernels, per_device(): pl.pallas_call(pack_kernel, out_shape=jax.ShapeDtypeStruct((peers * SENT,...  2.07 us
  transfers between devices with their start and end apart: 3, of which 1 were waited for; matrix products, arithmetic and copies ran while one was open for 3% of the time, Pallas kernels for 31%

profile of v4, /device:TPU:1, one launch (start us, length us, event | category | flops | bytes accessed | tf_op | source)
XLA Modules:
  0.0 89.8 jit_solution(5806814955341425938)
XLA Ops:
  0.0 2.1 %shard_map.82 = f32[1792,128]{1,0:T(8,128)} custom-call(s32[1]{0:T(128)} %bitcast.4.half_hi, s32[1]{0:T(128)} %bitcast.5.side, f32[3,128,128]{2,1,0:T(8,128)} %bitcast.82, f32[128,128]{1,0:T(8,128)} %bitcast.83, s32[128,128]{1,0:T(8,128)} %bitcast.84), custom_call_target="tpu_custom_call" | custom-call | tf_op jit(solution)/shard_map/pallas_call | solution.py:343
  2.1 0.0 copy-start.2
  2.1 0.0 copy-start.3
  2.1 0.0 copy-start.4
  2.1 0.0 copy-start.1
  2.1 0.0 copy-start
  2.1 8.7 %all-to-all-start = ((f32[32,56,128]{2,1,0:T(8,128)}), f32[32,56,128]{2,1,0:T(8,128)S(1)}, u32[]{:S(2)}, u32[]{:S(2)}) async-start(f32[32,56,128]{2,1,0:T(8,128)} %bitcast.80), calls=%async_computation | async-start | bytes 1835008 | tf_op jit(solution)/shard_map/all_to_all | solution.py:356
  10.9 0.0 copy-done.2
  11.0 0.7 convert_reduce_fusion.1
  13.1 0.2 select_reduce_fusion.1
  13.3 0.2 select_reduce_fusion
  13.5 0.0 copy-done.3
  13.5 0.0 copy-done.4
  13.6 0.1 stack.170
  13.7 0.1 copy.70
  13.9 0.1 stack.156
  14.0 0.1 copy.69
  14.1 0.1 pad.15.clone
  14.2 0.7 concatenate.23
  15.0 0.1 pad_add_fusion.1.steps
  15.1 0.0 copy-done.1
  15.1 0.1 maximum_bitcast_fusion
  15.2 0.0 copy-done
  15.2 10.8 %all-to-all-done.arrived = f32[32,56,128]{2,1,0:T(8,128)S(1)} async-done(((f32[32,56,128]{2,1,0:T(8,128)}), f32[32,56,128]{2,1,0:T(8,128)S(1)}, u32[]{:S(2)}, u32[]{:S(2)}) %all-to-all-start) | async-done | bytes 917536 | tf_op jit(solution)/shard_map/all_to_all | solution.py:356
  26.0 1.0 %shard_map.83.region = f32[241,8,128]{2,1,0:T(8,128)S(1)} custom-call(f32[32,56,128]{2,1,0:T(8,128)S(1)} %all-to-all-done.arrived), custom_call_target="tpu_custom_call" | custom-call | tf_op jit(solution)/shard_map/pallas_call | solution.py:361
  27.1 3.8 %collective-permute-start.1 = (f32[60,8,128]{2,1,0:T(8,128)S(1)}, f32[60,8,128]{2,1,0:T(8,128)S(1)}, u32[]{:S(2)}, u32[]{:S(2)}) collective-permute-start(f32[60,8,128]{2,1,0:T(8,128)S(1)} %get-tuple-element.31), channel_id=1, source_target_pairs={{32,0},{64,32},{96,64},{0,96},{33,1},{65,33},{97,65},{1,97},{34,2}... | collective-permute-start | bytes 737288 | tf_op jit(solution)/shard_map/ppermute | solution.py:372
  30.9 0.0 collective-permute-start
  30.9 28.2 %shard_map.84 = (f32[129,16,128]{2,1,0:T(8,128)S(1)}, bf16[128,128,128]{2,1,0:T(8,128)(2,1)S(1)}, bf16[128,128,128]{2,1,0:T(8,128)(2,1)S(1)}) custom-call(s32[2]{0:T(128)S(1)} %pad_add_fusion.1.steps, s32[3,528]{1,0:T(4,128)S(1)} %pad_add_fusion.ids, f32[241,8,128]{2,1,0:T(8,128)S(1)} %shard_map.83.region, bf16[96,256]{1,0:T(8,128)(2,1)S(1)} %fusion.4.w_home, ...), custom_call_target="tpu_custom_call" | custom-call | flops 10000000000 | bytes 10000000 | tf_op jit(solution)/shard_map/pallas_call | solution.py:385
  59.1 0.0 collective-permute-done.1.high
  59.1 0.0 collective-permute-done.low
  59.1 7.5 %shard_map.85 = (f32[32,12,128]{2,1,0:T(8,128)S(1)}, f32[129,16,128]{2,1,0:T(8,128)S(1)}) custom-call(s32[2]{0:T(128)S(1)} %pad_add_fusion.1.steps, s32[3,528]{1,0:T(4,128)S(1)} %pad_add_fusion.ids, f32[60,8,128]{2,1,0:T(8,128)S(1)} %collective-permute-done.low, f32[60,8,128]{2,1,0:T(8,128)S(1)} %collective-permute-done.1.high, ...), custom_call_target="tpu_custom_call", output_to_operand_aliasing={{1}: (8, {})} | custom-call | tf_op jit(solution)/shard_map/pallas_call | solution.py:394
  66.6 22.4 %all_to_all.10 = f32[32,12,128]{2,1,0:T(8,128)S(1)} all-to-all(f32[32,12,128]{2,1,0:T(8,128)S(1)} %get-tuple-element.12), channel_id=1, replica_groups=mesh['gx'=4,'gy'=4,'gz'=8] {'gy','gz'}, dimensions={0} | all-to-all | bytes 393216 | tf_op jit(solution)/shard_map/all_to_all | solution.py:403
  89.0 0.1 copy.73
  89.1 0.7 copy.74
  (24 shorter events, 0.3 us)
Async XLA Ops:
  2.1 8.8 %copy-start.2 = (s32[1,1,1,2,512]{4,3,2,1,0:T(2,128)S(1)}, s32[1,1,1,2,512]{4,3,2,1,0:T(2,128)}, u32[]{:S(2)}) copy-start(s32[1,1,1,2,512]{4,3,2,1,0:T(2,128)} %param.13) | copy-start | bytes 12292
  2.1 11.4 %copy-start.3 = (f32[64]{0:T(128)S(1)}, f32[64]{0:T(128)}, u32[]{:S(2)}) copy-start(f32[64]{0:T(128)} %param.11) | copy-start | bytes 772
  2.1 11.4 %copy-start.4 = (f32[64]{0:T(128)S(1)}, f32[64]{0:T(128)}, u32[]{:S(2)}) copy-start(f32[64]{0:T(128)} %param.12) | copy-start | bytes 772
  2.1 12.9 %copy-start.1 = (bf16[80,96]{1,0:T(8,128)(2,1)S(1)}, bf16[80,96]{1,0:T(8,128)(2,1)}, u32[]{:S(2)}) copy-start(bf16[80,96]{1,0:T(8,128)(2,1)} %constant.240) | copy-start | bytes 46084
  2.1 13.1 %copy-start = (bf16[96,128]{1,0:T(8,128)(2,1)S(1)}, bf16[96,128]{1,0:T(8,128)(2,1)}, u32[]{:S(2)}) copy-start(bf16[96,128]{1,0:T(8,128)(2,1)} %constant.241) | copy-start | bytes 73732
  2.1 23.9 %all-to-all-start = ((f32[32,56,128]{2,1,0:T(8,128)}), f32[32,56,128]{2,1,0:T(8,128)S(1)}, u32[]{:S(2)}, u32[]{:S(2)}) async-start(f32[32,56,128]{2,1,0:T(8,128)} %bitcast.80), calls=%async_computation | async-start | bytes 1835008 | tf_op jit(solution)/shard_map/all_to_all | solution.py:356
  27.1 32.0 %collective-permute-start.1 = (f32[60,8,128]{2,1,0:T(8,128)S(1)}, f32[60,8,128]{2,1,0:T(8,128)S(1)}, u32[]{:S(2)}, u32[]{:S(2)}) collective-permute-start(f32[60,8,128]{2,1,0:T(8,128)S(1)} %get-tuple-element.31), channel_id=1, source_target_pairs={{32,0},{64,32},{96,64},{0,96},{33,1},{65,33},{97,65},{1,97},{34,2}... | collective-permute-start | bytes 737288 | tf_op jit(solution)/shard_map/ppermute | solution.py:372
  30.9 28.2 %collective-permute-start = (f32[60,8,128]{2,1,0:T(8,128)S(1)}, f32[60,8,128]{2,1,0:T(8,128)S(1)}, u32[]{:S(2)}, u32[]{:S(2)}) collective-permute-start(f32[60,8,128]{2,1,0:T(8,128)S(1)} %get-tuple-element.32), channel_id=1, source_target_pairs={{0,32},{32,64},{64,96},{96,0},{1,33},{33,65},{65,97},{97,1},{2,34}... | collective-permute-start | bytes 737288 | tf_op jit(solution)/shard_map/ppermute | solution.py:371

commit v5 on v4

--- a/solution.py
+++ b/solution.py
@@ -225,12 +225,13 @@
         push = push.reshape(128, 128)
         high = push.astype(BF16)
         low = (push - high.astype(F32)).astype(BF16)
-        acc[h] += lax.dot_general(
+        once = lax.dot_general(
             rr[j],
             jnp.concatenate([high, low], 1),
             (((1,), (1,)), ((), ())),
             preferred_element_type=F32,
         )
+        acc[h] += once * ids[3, batch * BATCH + q].astype(F32)
 
     def both(buf_next, buf_now, batch_next, batch_now):
         for q in range(BATCH):
@@ -314,11 +315,15 @@
     plane = place_y * (LAYERS + 2) + place_z
     side = jnp.where(step_x == 0, member // (GRID * LAYERS), (step_x + 1) // 2)
     listed = home >= 0
-    near = listed & (step_x == 0)
-    far = listed & (step_x != 0)
     unit = 2 * BATCH
     order = jnp.arange(home.shape[0])
     upto = order[None, :] <= order[:, None]
+    key = home * (27 * blocks) + source
+    same = key[None, :] == key[:, None]
+    times = jnp.sum(jnp.where(same, 1, 0), 1)
+    first = jnp.sum(jnp.where(same & upto, 1, 0), 1) == 1
+    near = listed & first & (step_x == 0)
+    far = listed & first & (step_x != 0)
     near_at = jnp.sum(jnp.where(upto & near[None, :], 1, 0), 1)
     far_at = jnp.sum(jnp.where(upto & far[None, :], 1, 0), 1)
     near_steps = (jnp.sum(near.astype(jnp.int32)) + unit - 1) // unit
@@ -327,9 +332,10 @@
     code = home * 256 + side * 60 + plane + 1
     slots = jnp.arange(home.shape[0] + 2 * unit)
     found = jnp.sum(jnp.where(slots[:, None] == at[None, :], code[None, :], 0), 1)
+    times = jnp.sum(jnp.where(slots[:, None] == at[None, :], times[None, :], 0), 1)
     real = found > 0
     code = jnp.maximum(found - 1, 0)
-    ids = jnp.stack([code // 256, code % 256, jnp.where(real, code // 256, blocks)])
+    ids = jnp.stack([code // 256, code % 256, jnp.where(real, code // 256, blocks), times])
     return jnp.stack([near_steps, far_steps]), ids
 
 

time: 89.2 us -> 87.1 us (0.976); the launches traced: 89.8 us -> 86.3 us
  blocking collectives: 22.4 us -> 16.4 us
  Pallas kernels: 38.8 us -> 41.4 us
  other arithmetic: 1.56 us -> 2.65 us
  waiting for transfers between devices: 10.8 us -> 9.71 us
    all_to_all x1, blocking collectives: 22.4 us -> 16.4 us  [per_device(): lax.all_to_all(totals, ('gy', 'gz'), split_axis=0, concat_axis=0, tiled=T...]
    pallas_call x1, Pallas kernels: 28.2 us -> 30.3 us  [per_device(): pl.pallas_call(near_kernel, out_shape=[acc_shape, factor_shape, factor_sh...]
    all_to_all x1, waiting for transfers between devices: 10.8 us -> 9.71 us  [per_device(): lax.all_to_all(outgoing.reshape(peers, SENT, width), ('gy', 'gz'), split_...]
    reduce_sum x0 -> x2, other arithmetic: none -> 1 us  [the longest x1 0.63 us: tile_lists(): far_steps = (jnp.sum(far.astype(jnp.int32)) + unit - 1) // unit]
  transfers between devices with their start and end apart: 3 -> 3, of which waited for: 1 -> 1; matrix products, arithmetic and copies ran while one was open for 3% -> 5% of each run, Pallas kernels for 31% -> 35%
where the time goes in v5:
time: 87.1 us; the launch traced here: 86.3 us
  Pallas kernels  41.4 us (48%)
  blocking collectives  16.4 us (19%)
  starting transfers between devices  12.6 us (14%)
  waiting for transfers between devices  9.71 us (11%)
  other arithmetic  2.65 us (3%)
  local copies, waits for them, and re-layouts  2.07 us (2%)
  between operations  1.62 us (2%)
    pallas_call x1, Pallas kernels, per_device(): pl.pallas_call(near_kernel, out_shape=[acc_shape, factor_shape, factor_sh...  30.3 us
    all_to_all x1, blocking collectives, per_device(): lax.all_to_all(totals, ('gy', 'gz'), split_axis=0, concat_axis=0, tiled=T...  16.4 us
    all_to_all x1, waiting for transfers between devices, per_device(): lax.all_to_all(outgoing.reshape(peers, SENT, width), ('gy', 'gz'), split_...  9.71 us
    all_to_all x1, starting transfers between devices, per_device(): lax.all_to_all(outgoing.reshape(peers, SENT, width), ('gy', 'gz'), split_...  8.74 us
    pallas_call x1, Pallas kernels, per_device(): pl.pallas_call(far_kernel, out_shape=[jax.ShapeDtypeStruct((peers, 12, wi...  8 us
    ppermute x1, starting transfers between devices, per_device(): high = lax.ppermute(region[:60], 'gx', backward)  3.83 us
    pallas_call x1, Pallas kernels, per_device(): pl.pallas_call(pack_kernel, out_shape=jax.ShapeDtypeStruct((peers * SENT,...  2.04 us
  transfers between devices with their start and end apart: 3, of which 1 were waited for; matrix products, arithmetic and copies ran while one was open for 5% of the time, Pallas kernels for 35%

profile of v5, /device:TPU:1, one launch (start us, length us, event | category | flops | bytes accessed | tf_op | source)
XLA Modules:
  0.0 86.3 jit_solution(15926330508619164704)
XLA Ops:
  0.0 2.0 %shard_map.82 = f32[1792,128]{1,0:T(8,128)} custom-call(s32[1]{0:T(128)} %bitcast.5.half_hi, s32[1]{0:T(128)} %bitcast.6.side, f32[3,128,128]{2,1,0:T(8,128)} %bitcast.83, f32[128,128]{1,0:T(8,128)} %bitcast.84, s32[128,128]{1,0:T(8,128)} %bitcast.85), custom_call_target="tpu_custom_call" | custom-call | tf_op jit(solution)/shard_map/pallas_call | solution.py:349
  2.0 0.0 copy-start.2
  2.1 0.0 copy-start.3
  2.1 0.0 copy-start.4
  2.1 0.0 copy-start.1
  2.1 0.0 copy-start
  2.1 8.7 %all-to-all-start = ((f32[32,56,128]{2,1,0:T(8,128)}), f32[32,56,128]{2,1,0:T(8,128)S(1)}, u32[]{:S(2)}, u32[]{:S(2)}) async-start(f32[32,56,128]{2,1,0:T(8,128)} %bitcast.81), calls=%async_computation | async-start | bytes 1835008 | tf_op jit(solution)/shard_map/all_to_all | solution.py:362
  10.9 0.0 copy-done.2
  10.9 0.4 fusion
  11.3 0.6 convert_reduce_fusion.1
  12.6 0.6 convert_reduce_fusion
  13.9 0.2 select_reduce_fusion.2
  14.2 0.4 select_reduce_fusion.1
  14.6 0.0 copy-done.3
  14.6 0.0 copy-done.4
  14.7 0.1 stack.174
  14.7 0.1 copy.70
  14.9 0.1 stack.160
  15.1 0.1 copy.69
  15.2 0.1 pad.15.clone
  15.3 0.7 concatenate.23
  16.0 0.1 pad_add_fusion.1.steps
  16.1 0.0 copy-done.1
  16.2 0.1 maximum_bitcast_fusion
  16.2 0.0 copy-done
  16.3 9.7 %all-to-all-done.arrived = f32[32,56,128]{2,1,0:T(8,128)S(1)} async-done(((f32[32,56,128]{2,1,0:T(8,128)}), f32[32,56,128]{2,1,0:T(8,128)S(1)}, u32[]{:S(2)}, u32[]{:S(2)}) %all-to-all-start) | async-done | bytes 917536 | tf_op jit(solution)/shard_map/all_to_all | solution.py:362
  26.0 1.0 %shard_map.83.region = f32[241,8,128]{2,1,0:T(8,128)S(1)} custom-call(f32[32,56,128]{2,1,0:T(8,128)S(1)} %all-to-all-done.arrived), custom_call_target="tpu_custom_call" | custom-call | tf_op jit(solution)/shard_map/pallas_call | solution.py:367
  27.1 3.8 %collective-permute-start.1 = (f32[60,8,128]{2,1,0:T(8,128)S(1)}, f32[60,8,128]{2,1,0:T(8,128)S(1)}, u32[]{:S(2)}, u32[]{:S(2)}) collective-permute-start(f32[60,8,128]{2,1,0:T(8,128)S(1)} %get-tuple-element.36), channel_id=1, source_target_pairs={{32,0},{64,32},{96,64},{0,96},{33,1},{65,33},{97,65},{1,97},{34,2}... | collective-permute-start | bytes 737288 | tf_op jit(solution)/shard_map/ppermute | solution.py:378
  30.9 0.0 collective-permute-start
  30.9 30.3 %shard_map.84 = (f32[129,16,128]{2,1,0:T(8,128)S(1)}, bf16[128,128,128]{2,1,0:T(8,128)(2,1)S(1)}, bf16[128,128,128]{2,1,0:T(8,128)(2,1)S(1)}) custom-call(s32[2]{0:T(128)S(1)} %pad_add_fusion.1.steps, s32[4,528]{1,0:T(4,128)S(1)} %pad_add_fusion.ids, f32[241,8,128]{2,1,0:T(8,128)S(1)} %shard_map.83.region, bf16[96,256]{1,0:T(8,128)(2,1)S(1)} %fusion.5.w_home, ...), custom_call_target="tpu_custom_call" | custom-call | flops 10000000000 | bytes 10000000 | tf_op jit(solution)/shard_map/pallas_call | solution.py:391
  61.2 0.0 collective-permute-done.1.high
  61.2 0.0 collective-permute-done.low
  61.2 8.0 %shard_map.85 = (f32[32,12,128]{2,1,0:T(8,128)S(1)}, f32[129,16,128]{2,1,0:T(8,128)S(1)}) custom-call(s32[2]{0:T(128)S(1)} %pad_add_fusion.1.steps, s32[4,528]{1,0:T(4,128)S(1)} %pad_add_fusion.ids, f32[60,8,128]{2,1,0:T(8,128)S(1)} %collective-permute-done.low, f32[60,8,128]{2,1,0:T(8,128)S(1)} %collective-permute-done.1.high, ...), custom_call_target="tpu_custom_call", output_to_operand_aliasing={{1}: (8, {})} | custom-call | tf_op jit(solution)/shard_map/pallas_call | solution.py:400
  69.2 16.4 %all_to_all.10 = f32[32,12,128]{2,1,0:T(8,128)S(1)} all-to-all(f32[32,12,128]{2,1,0:T(8,128)S(1)} %get-tuple-element.12), channel_id=1, replica_groups=mesh['gx'=4,'gy'=4,'gz'=8] {'gy','gz'}, dimensions={0} | all-to-all | bytes 393216 | tf_op jit(solution)/shard_map/all_to_all | solution.py:409
  85.6 0.1 copy.73
  85.7 0.7 copy.74
  (25 shorter events, 0.3 us)
Async XLA Ops:
  2.0 8.8 %copy-start.2 = (s32[1,1,1,2,512]{4,3,2,1,0:T(2,128)S(1)}, s32[1,1,1,2,512]{4,3,2,1,0:T(2,128)}, u32[]{:S(2)}) copy-start(s32[1,1,1,2,512]{4,3,2,1,0:T(2,128)} %param.13) | copy-start | bytes 12292
  2.1 12.5 %copy-start.3 = (f32[64]{0:T(128)S(1)}, f32[64]{0:T(128)}, u32[]{:S(2)}) copy-start(f32[64]{0:T(128)} %param.11) | copy-start | bytes 772
  2.1 12.5 %copy-start.4 = (f32[64]{0:T(128)S(1)}, f32[64]{0:T(128)}, u32[]{:S(2)}) copy-start(f32[64]{0:T(128)} %param.12) | copy-start | bytes 772
  2.1 14.0 %copy-start.1 = (bf16[80,96]{1,0:T(8,128)(2,1)S(1)}, bf16[80,96]{1,0:T(8,128)(2,1)}, u32[]{:S(2)}) copy-start(bf16[80,96]{1,0:T(8,128)(2,1)} %constant.242) | copy-start | bytes 46084
  2.1 14.1 %copy-start = (bf16[96,128]{1,0:T(8,128)(2,1)S(1)}, bf16[96,128]{1,0:T(8,128)(2,1)}, u32[]{:S(2)}) copy-start(bf16[96,128]{1,0:T(8,128)(2,1)} %constant.243) | copy-start | bytes 73732
  2.1 23.9 %all-to-all-start = ((f32[32,56,128]{2,1,0:T(8,128)}), f32[32,56,128]{2,1,0:T(8,128)S(1)}, u32[]{:S(2)}, u32[]{:S(2)}) async-start(f32[32,56,128]{2,1,0:T(8,128)} %bitcast.81), calls=%async_computation | async-start | bytes 1835008 | tf_op jit(solution)/shard_map/all_to_all | solution.py:362
  27.1 34.1 %collective-permute-start.1 = (f32[60,8,128]{2,1,0:T(8,128)S(1)}, f32[60,8,128]{2,1,0:T(8,128)S(1)}, u32[]{:S(2)}, u32[]{:S(2)}) collective-permute-start(f32[60,8,128]{2,1,0:T(8,128)S(1)} %get-tuple-element.36), channel_id=1, source_target_pairs={{32,0},{64,32},{96,64},{0,96},{33,1},{65,33},{97,65},{1,97},{34,2}... | collective-permute-start | bytes 737288 | tf_op jit(solution)/shard_map/ppermute | solution.py:378
  30.9 30.3 %collective-permute-start = (f32[60,8,128]{2,1,0:T(8,128)S(1)}, f32[60,8,128]{2,1,0:T(8,128)S(1)}, u32[]{:S(2)}, u32[]{:S(2)}) collective-permute-start(f32[60,8,128]{2,1,0:T(8,128)S(1)} %get-tuple-element.37), channel_id=1, source_target_pairs={{0,32},{32,64},{64,96},{96,0},{1,33},{33,65},{65,97},{97,1},{2,34}... | collective-permute-start | bytes 737288 | tf_op jit(solution)/shard_map/ppermute | solution.py:377

commit v6 on v5

--- a/solution.py
+++ b/solution.py
@@ -15,9 +15,14 @@
 LAYERS = 8
 CELL = 11.0
 LIMIT = 97.0
-COULOMB = 332.0636
+SCALE = LIMIT**-0.5
+SOFT = 16.0 / LIMIT
+COULOMB = 332.0636 / LIMIT
+FACTOR_12 = 48.0 * LIMIT**-6.5
+FACTOR_6 = 24.0 * LIMIT**-3.5
 
 ROW_X, ROW_Y, ROW_Z, ROW_C, ROW_TYPE, ROW_Q, ROW_ONE, ROW_CC = range(8)
+ROW_SOFT = ROW_TYPE
 TYPES = 64
 ORDER = 13
 NX = 32
@@ -45,16 +50,13 @@
             src_w[at, term(row, j)] = -2.0
             at += 1
     for part in range(3):
-        home[term(ROW_Q, part), at] = 1.0
+        home[term(ROW_SOFT, part), at] = 1.0
         src_w[at, term(ROW_ONE, 0)] = 1.0
         at += 1
     for part in range(3):
         home[term(ROW_ONE, 0), at] = 1.0
         src_w[at, term(ROW_Q, part)] = 1.0
         at += 1
-    home[term(ROW_ONE, 0), at] = 1.0
-    src_w[at, term(ROW_ONE, 0)] = 16.0
-    at += 1
     for i, j in ((0, 0), (0, 1), (1, 0), (1, 1), (0, 2), (2, 0)):
         home[term(ROW_CC, i), at] = 1.0
         src_c[at, term(ROW_C, j)] = 1.0
@@ -80,9 +82,9 @@
 
     h_high, h_low = halves(jnp.stack([root * p for p in powers]))
     zero = jnp.zeros_like(half)
-    p12 = jnp.stack([root * powers[12 - k] * (48.0 * math.comb(12, k)) for k in range(ORDER)])
+    p12 = jnp.stack([root * powers[12 - k] * (FACTOR_12 * math.comb(12, k)) for k in range(ORDER)])
     p6 = jnp.stack(
-        [root * powers[6 - k] * (24.0 * math.comb(6, k)) if k <= 6 else zero for k in range(ORDER)]
+        [root * powers[6 - k] * (FACTOR_6 * math.comb(6, k)) if k <= 6 else zero for k in range(ORDER)]
     )
     pad = jnp.zeros((NY - 3 * ORDER, TYPES), F32)
     home_y = jnp.concatenate([h_high, h_high, h_low, pad])
@@ -156,18 +158,11 @@
             off_y = place_y.astype(F32) * CELL - 3 * CELL
             off_z = place_z.astype(F32) * CELL - 5 * CELL
             off = jnp.where(row == ROW_X, off_x, 0.0) + jnp.where(row == ROW_Y, off_y, 0.0)
-            out[place] = block + (off + jnp.where(row == ROW_Z, off_z, 0.0))
+            block = block + (off + jnp.where(row == ROW_Z, off_z, 0.0))
+            out[place] = block * jnp.where(row < 3, SCALE, 1.0)
         return carry
 
     lax.fori_loop(0, 32, body, 0, unroll=2)
-
-
-def powers_of(w):
-    u = lax.rsqrt(w)
-    inv = u * u
-    inv2 = inv * inv
-    inv4 = inv2 * inv2
-    return inv4 * (inv2 * inv), inv4, u * inv
 
 
 def factors(block, off_x=None):
@@ -176,6 +171,7 @@
     moved = block if off_x is None else block + jnp.where(row == ROW_X, off_x, 0.0)
     square = jnp.sum(jnp.where(row < 3, moved * moved, 0.0), axis=0, keepdims=True)
     moved = jnp.where(row == ROW_Q, square, jnp.where(row == ROW_ONE, 1.0, moved))
+    moved = jnp.where(row == ROW_SOFT, square + SOFT, moved)
     moved = jnp.where(row == ROW_CC, COULOMB * block[ROW_C : ROW_C + 1], moved)
     high = moved.astype(BF16).astype(F32)
     rest = moved - high
@@ -207,8 +203,6 @@
 
 
 def all_tiles(first, pairs, ids, lx, ly, rx, ry, rr, acc, buf_a, buf_b):
-    k7, k4, k3 = powers_of(jnp.full((8, 128), LIMIT, F32))
-
     def quantities(buf, batch, q):
         h, j = ids[0, batch * BATCH + q], ids[1, batch * BATCH + q]
         buf[q, 0] = jnp.dot(lx[h][:, :NX], rx[j], preferred_element_type=F32)
@@ -220,8 +214,11 @@
         def part(i, side):
             return buf[q, i, :, 128 * side : 128 * side + 128].reshape(16, 8, 128)
 
-        p7, p4, p3 = powers_of(jnp.minimum(part(0, 0), LIMIT))
-        push = (p7 - k7) * part(1, 0) - (p4 - k4) * part(1, 1) + (p3 - k3) * part(0, 1)
+        u = lax.rsqrt(jnp.minimum(part(0, 0), 1.0))
+        inv = u * u
+        inv3 = inv * inv * inv
+        c12, c6, charge = part(1, 0), part(1, 1), part(0, 1)
+        push = inv * (inv3 * (inv3 * c12 - c6) + u * charge) - ((c12 - c6) + charge)
         push = push.reshape(128, 128)
         high = push.astype(BF16)
         low = (push - high.astype(F32)).astype(BF16)
@@ -287,7 +284,7 @@
     def prepare(i, carry):
         for k, (plane, off_x) in enumerate(((low, -44.0), (high, 44.0))):
             places = [i * FAR_GROUP + g for g in range(FAR_GROUP)]
-            z = jnp.concatenate([factors(plane[p], off_x) for p in places], 1)
+            z = jnp.concatenate([factors(plane[p], off_x * SCALE) for p in places], 1)
             store_source([p + 60 * k for p in places], z, w_src, rx, ry, rr)
         return carry
 

time: 87.1 us -> 86.6 us (level)
  Pallas kernels: 41.4 us -> 40.4 us
  blocking collectives: 16.4 us -> 17.4 us
    all_to_all x1, blocking collectives: 16.4 us -> 17.4 us  [per_device(): lax.all_to_all(totals, ('gy', 'gz'), split_axis=0, concat_axis=0, tiled=T...]
    pallas_call x1, Pallas kernels: 30.3 us -> 29.4 us  [per_device(): pl.pallas_call(near_kernel, out_shape=[acc_shape, factor_shape, factor_sh...]
  transfers between devices with their start and end apart: 3 -> 3, of which waited for: 1 -> 1; matrix products, arithmetic and copies ran while one was open for 5% -> 5% of each run, Pallas kernels for 35% -> 34%
where the time goes in v6:
time: 86.6 us; the launch traced here: 86.3 us
  Pallas kernels  40.4 us (47%)
  blocking collectives  17.4 us (20%)
  starting transfers between devices  12.6 us (15%)
  waiting for transfers between devices  9.71 us (11%)
  other arithmetic  2.65 us (3%)
  local copies, waits for them, and re-layouts  2.07 us (2%)
  between operations  1.61 us (2%)
    pallas_call x1, Pallas kernels, per_device(): pl.pallas_call(near_kernel, out_shape=[acc_shape, factor_shape, factor_sh...  29.4 us
    all_to_all x1, blocking collectives, per_device(): lax.all_to_all(totals, ('gy', 'gz'), split_axis=0, concat_axis=0, tiled=T...  17.4 us
    all_to_all x1, waiting for transfers between devices, per_device(): lax.all_to_all(outgoing.reshape(peers, SENT, width), ('gy', 'gz'), split_...  9.71 us
    all_to_all x1, starting transfers between devices, per_device(): lax.all_to_all(outgoing.reshape(peers, SENT, width), ('gy', 'gz'), split_...  8.74 us
    pallas_call x1, Pallas kernels, per_device(): pl.pallas_call(far_kernel, out_shape=[jax.ShapeDtypeStruct((peers, 12, wi...  7.82 us
    ppermute x1, starting transfers between devices, per_device(): high = lax.ppermute(region[:60], 'gx', backward)  3.83 us
    pallas_call x1, Pallas kernels, per_device(): pl.pallas_call(pack_kernel, out_shape=jax.ShapeDtypeStruct((peers * SENT,...  2.04 us
  transfers between devices with their start and end apart: 3, of which 1 were waited for; matrix products, arithmetic and copies ran while one was open for 5% of the time, Pallas kernels for 34%

profile of v6, /device:TPU:1, one launch (start us, length us, event | category | flops | bytes accessed | tf_op | source)
XLA Modules:
  0.0 86.3 jit_solution(13862969725881592999)
XLA Ops:
  0.0 2.0 %shard_map.82 = f32[1792,128]{1,0:T(8,128)} custom-call(s32[1]{0:T(128)} %bitcast.5.half_hi, s32[1]{0:T(128)} %bitcast.6.side, f32[3,128,128]{2,1,0:T(8,128)} %bitcast.83, f32[128,128]{1,0:T(8,128)} %bitcast.84, s32[128,128]{1,0:T(8,128)} %bitcast.85), custom_call_target="tpu_custom_call" | custom-call | tf_op jit(solution)/shard_map/pallas_call | solution.py:346
  2.0 0.0 copy-start.2
  2.1 0.0 copy-start.3
  2.1 0.0 copy-start.4
  2.1 0.0 copy-start.1
  2.1 0.0 copy-start
  2.1 8.7 %all-to-all-start = ((f32[32,56,128]{2,1,0:T(8,128)}), f32[32,56,128]{2,1,0:T(8,128)S(1)}, u32[]{:S(2)}, u32[]{:S(2)}) async-start(f32[32,56,128]{2,1,0:T(8,128)} %bitcast.81), calls=%async_computation | async-start | bytes 1835008 | tf_op jit(solution)/shard_map/all_to_all | solution.py:359
  10.9 0.0 copy-done.2
  10.9 0.4 fusion
  11.3 0.6 convert_reduce_fusion.1
  12.6 0.6 convert_reduce_fusion
  13.9 0.2 select_reduce_fusion.2
  14.2 0.4 select_reduce_fusion.1
  14.6 0.0 copy-done.3
  14.6 0.0 copy-done.4
  14.7 0.1 stack.174
  14.7 0.1 copy.70
  14.9 0.1 stack.160
  15.1 0.1 copy.69
  15.2 0.1 pad.15.clone
  15.3 0.7 concatenate.23
  16.0 0.1 pad_add_fusion.1.steps
  16.1 0.0 copy-done.1
  16.2 0.1 maximum_bitcast_fusion
  16.2 0.0 copy-done
  16.3 9.7 %all-to-all-done.arrived = f32[32,56,128]{2,1,0:T(8,128)S(1)} async-done(((f32[32,56,128]{2,1,0:T(8,128)}), f32[32,56,128]{2,1,0:T(8,128)S(1)}, u32[]{:S(2)}, u32[]{:S(2)}) %all-to-all-start) | async-done | bytes 917536 | tf_op jit(solution)/shard_map/all_to_all | solution.py:359
  26.0 1.1 %shard_map.83.region = f32[241,8,128]{2,1,0:T(8,128)S(1)} custom-call(f32[32,56,128]{2,1,0:T(8,128)S(1)} %all-to-all-done.arrived), custom_call_target="tpu_custom_call" | custom-call | tf_op jit(solution)/shard_map/pallas_call | solution.py:364
  27.1 3.8 %collective-permute-start.1 = (f32[60,8,128]{2,1,0:T(8,128)S(1)}, f32[60,8,128]{2,1,0:T(8,128)S(1)}, u32[]{:S(2)}, u32[]{:S(2)}) collective-permute-start(f32[60,8,128]{2,1,0:T(8,128)S(1)} %get-tuple-element.36), channel_id=1, source_target_pairs={{32,0},{64,32},{96,64},{0,96},{33,1},{65,33},{97,65},{1,97},{34,2}... | collective-permute-start | bytes 737288 | tf_op jit(solution)/shard_map/ppermute | solution.py:375
  31.0 0.0 collective-permute-start
  31.0 29.4 %shard_map.84 = (f32[129,16,128]{2,1,0:T(8,128)S(1)}, bf16[128,128,128]{2,1,0:T(8,128)(2,1)S(1)}, bf16[128,128,128]{2,1,0:T(8,128)(2,1)S(1)}) custom-call(s32[2]{0:T(128)S(1)} %pad_add_fusion.1.steps, s32[4,528]{1,0:T(4,128)S(1)} %pad_add_fusion.ids, f32[241,8,128]{2,1,0:T(8,128)S(1)} %shard_map.83.region, bf16[96,256]{1,0:T(8,128)(2,1)S(1)} %fusion.5.w_home, ...), custom_call_target="tpu_custom_call" | custom-call | flops 10000000000 | bytes 10000000 | tf_op jit(solution)/shard_map/pallas_call | solution.py:388
  60.4 0.0 collective-permute-done.1.high
  60.4 0.0 collective-permute-done.low
  60.4 7.8 %shard_map.85 = (f32[32,12,128]{2,1,0:T(8,128)S(1)}, f32[129,16,128]{2,1,0:T(8,128)S(1)}) custom-call(s32[2]{0:T(128)S(1)} %pad_add_fusion.1.steps, s32[4,528]{1,0:T(4,128)S(1)} %pad_add_fusion.ids, f32[60,8,128]{2,1,0:T(8,128)S(1)} %collective-permute-done.low, f32[60,8,128]{2,1,0:T(8,128)S(1)} %collective-permute-done.1.high, ...), custom_call_target="tpu_custom_call", output_to_operand_aliasing={{1}: (8, {})} | custom-call | tf_op jit(solution)/shard_map/pallas_call | solution.py:397
  68.2 17.4 %all_to_all.10 = f32[32,12,128]{2,1,0:T(8,128)S(1)} all-to-all(f32[32,12,128]{2,1,0:T(8,128)S(1)} %get-tuple-element.12), channel_id=1, replica_groups=mesh['gx'=4,'gy'=4,'gz'=8] {'gy','gz'}, dimensions={0} | all-to-all | bytes 393216 | tf_op jit(solution)/shard_map/all_to_all | solution.py:406
  85.6 0.1 copy.73
  85.6 0.7 copy.74
  (25 shorter events, 0.3 us)
Async XLA Ops:
  2.0 8.8 %copy-start.2 = (s32[1,1,1,2,512]{4,3,2,1,0:T(2,128)S(1)}, s32[1,1,1,2,512]{4,3,2,1,0:T(2,128)}, u32[]{:S(2)}) copy-start(s32[1,1,1,2,512]{4,3,2,1,0:T(2,128)} %param.13) | copy-start | bytes 12292
  2.1 12.5 %copy-start.3 = (f32[64]{0:T(128)S(1)}, f32[64]{0:T(128)}, u32[]{:S(2)}) copy-start(f32[64]{0:T(128)} %param.11) | copy-start | bytes 772
  2.1 12.5 %copy-start.4 = (f32[64]{0:T(128)S(1)}, f32[64]{0:T(128)}, u32[]{:S(2)}) copy-start(f32[64]{0:T(128)} %param.12) | copy-start | bytes 772
  2.1 14.0 %copy-start.1 = (bf16[80,96]{1,0:T(8,128)(2,1)S(1)}, bf16[80,96]{1,0:T(8,128)(2,1)}, u32[]{:S(2)}) copy-start(bf16[80,96]{1,0:T(8,128)(2,1)} %constant.242) | copy-start | bytes 46084
  2.1 14.1 %copy-start = (bf16[96,128]{1,0:T(8,128)(2,1)S(1)}, bf16[96,128]{1,0:T(8,128)(2,1)}, u32[]{:S(2)}) copy-start(bf16[96,128]{1,0:T(8,128)(2,1)} %constant.243) | copy-start | bytes 73732
  2.1 23.9 %all-to-all-start = ((f32[32,56,128]{2,1,0:T(8,128)}), f32[32,56,128]{2,1,0:T(8,128)S(1)}, u32[]{:S(2)}, u32[]{:S(2)}) async-start(f32[32,56,128]{2,1,0:T(8,128)} %bitcast.81), calls=%async_computation | async-start | bytes 1835008 | tf_op jit(solution)/shard_map/all_to_all | solution.py:359
  27.1 33.2 %collective-permute-start.1 = (f32[60,8,128]{2,1,0:T(8,128)S(1)}, f32[60,8,128]{2,1,0:T(8,128)S(1)}, u32[]{:S(2)}, u32[]{:S(2)}) collective-permute-start(f32[60,8,128]{2,1,0:T(8,128)S(1)} %get-tuple-element.36), channel_id=1, source_target_pairs={{32,0},{64,32},{96,64},{0,96},{33,1},{65,33},{97,65},{1,97},{34,2}... | collective-permute-start | bytes 737288 | tf_op jit(solution)/shard_map/ppermute | solution.py:375
  31.0 29.4 %collective-permute-start = (f32[60,8,128]{2,1,0:T(8,128)S(1)}, f32[60,8,128]{2,1,0:T(8,128)S(1)}, u32[]{:S(2)}, u32[]{:S(2)}) collective-permute-start(f32[60,8,128]{2,1,0:T(8,128)S(1)} %get-tuple-element.37), channel_id=1, source_target_pairs={{0,32},{32,64},{64,96},{96,0},{1,33},{33,65},{65,97},{97,1},{2,34}... | collective-permute-start | bytes 737288 | tf_op jit(solution)/shard_map/ppermute | solution.py:374

commit v7 on v6

--- a/solution.py
+++ b/solution.py
@@ -141,28 +141,27 @@
 
 def unpack_kernel(arrived, out):
     row = lax.broadcasted_iota(jnp.int32, (8, 128), 0)
-
-    def body(s, carry):
-        cell_x, cell_y, upper = s // 8, s // 2 % 4, s % 2
-        for c in range(10):
-            place_y = cell_y + 1
-            if c >= 5:
-                place_y = jnp.where(cell_y == 0, GRID + 1, 0)
-            place_z = upper * 4 + c % 5 + 1 if c % 5 < 4 else jnp.where(upper == 1, 0, LAYERS + 1)
-            place = (cell_x * (GRID + 2) + place_y) * (LAYERS + 2) + place_z
-            if c >= 5:
-                inner = jnp.logical_and(cell_y > 0, cell_y < GRID - 1)
-                place = jnp.where(inner, NEAR, place)
-            block = jnp.concatenate([arrived[s, 5 * c : 5 * c + 5], jnp.zeros((3, 128), F32)])
-            off_x = cell_x.astype(F32) * CELL - 2 * CELL
-            off_y = place_y.astype(F32) * CELL - 3 * CELL
-            off_z = place_z.astype(F32) * CELL - 5 * CELL
-            off = jnp.where(row == ROW_X, off_x, 0.0) + jnp.where(row == ROW_Y, off_y, 0.0)
-            block = block + (off + jnp.where(row == ROW_Z, off_z, 0.0))
-            out[place] = block * jnp.where(row < 3, SCALE, 1.0)
+    scale = jnp.where(row < 3, SCALE, 1.0)
+
+    def body(cell_x, carry):
+        off_x = (cell_x.astype(F32) - 2) * (CELL * SCALE)
+        for s in range(8):
+            cell_y, upper = s // 2, s % 2
+            for c in range(10 if cell_y in (0, GRID - 1) else 5):
+                place_y = cell_y + 1
+                if c >= 5:
+                    place_y = GRID + 1 if cell_y == 0 else 0
+                place_z = upper * 4 + c % 5 + 1 if c % 5 < 4 else (1 - upper) * (LAYERS + 1)
+                off_y = (place_y - 3) * (CELL * SCALE)
+                off_z = (place_z - 5) * (CELL * SCALE)
+                off = jnp.where(row == ROW_Y, off_y, jnp.where(row == ROW_Z, off_z, 0.0))
+                off = jnp.where(row == ROW_X, off_x, off)
+                rows = arrived[8 * cell_x + s, 5 * c : 5 * c + 5]
+                block = jnp.concatenate([rows, jnp.zeros((3, 128), F32)]) * scale + off
+                out[(cell_x * (GRID + 2) + place_y) * (LAYERS + 2) + place_z] = block
         return carry
 
-    lax.fori_loop(0, 32, body, 0, unroll=2)
+    lax.fori_loop(0, GRID, body, 0)
 
 
 def factors(block, off_x=None):
@@ -246,7 +245,12 @@
             both(buf_a, buf_b, jnp.minimum(2 * i + 2, last), 2 * i + 1)
             return carry
 
-        lax.fori_loop(first, first + pairs, body, 0)
+        def twice(i, carry):
+            body(first + 2 * i, carry)
+            return body(first + 2 * i + 1, carry)
+
+        lax.fori_loop(0, pairs // 2, twice, 0)
+        lax.fori_loop(first + pairs // 2 * 2, first + pairs, body, 0)
 
 
 def near_place(b):
@@ -363,7 +367,7 @@
     w_home, w_src = weights(lj_sigma, lj_epsilon)
     region = pl.pallas_call(
         unpack_kernel,
-        out_shape=jax.ShapeDtypeStruct((NEAR + 1, 8, width), F32),
+        out_shape=jax.ShapeDtypeStruct((NEAR, 8, width), F32),
         in_specs=[vmem],
         out_specs=vmem,
         compiler_params=small,

time: 86.6 us -> 80.1 us (0.925)
  Pallas kernels: 40.4 us -> 29.6 us
  blocking collectives: 17.4 us -> 21.8 us
    pallas_call x1, Pallas kernels: 29.4 us -> 21.1 us  [per_device(): pl.pallas_call(near_kernel, out_shape=[acc_shape, factor_shape, factor_sh...]
    all_to_all x1, blocking collectives: 17.4 us -> 21.8 us  [per_device(): lax.all_to_all(totals, ('gy', 'gz'), split_axis=0, concat_axis=0, tiled=T...]
    pallas_call x1, Pallas kernels: 7.82 us -> 6.32 us  [per_device(): pl.pallas_call(far_kernel, out_shape=[jax.ShapeDtypeStruct((peers, 12, wi...]
    pallas_call x1, Pallas kernels: 1.12 us -> 0.18 us  [per_device(): pl.pallas_call(unpack_kernel, out_shape=jax.ShapeDtypeStruct((NEAR, 8, wi...]
  transfers between devices with their start and end apart: 3 -> 3, of which waited for: 1 -> 1; matrix products, arithmetic and copies ran while one was open for 5% -> 5% of each run, Pallas kernels for 34% -> 26%
where the time goes in v7:
time: 80.1 us; the launch traced here: 80 us
  Pallas kernels  29.6 us (37%)
  blocking collectives  21.8 us (27%)
  starting transfers between devices  12.6 us (16%)
  waiting for transfers between devices  9.71 us (12%)
  other arithmetic  2.65 us (3%)
  local copies, waits for them, and re-layouts  2.07 us (3%)
  between operations  1.61 us (2%)
    all_to_all x1, blocking collectives, per_device(): lax.all_to_all(totals, ('gy', 'gz'), split_axis=0, concat_axis=0, tiled=T...  21.8 us
    pallas_call x1, Pallas kernels, per_device(): pl.pallas_call(near_kernel, out_shape=[acc_shape, factor_shape, factor_sh...  21.1 us
    all_to_all x1, waiting for transfers between devices, per_device(): lax.all_to_all(outgoing.reshape(peers, SENT, width), ('gy', 'gz'), split_...  9.71 us
    all_to_all x1, starting transfers between devices, per_device(): lax.all_to_all(outgoing.reshape(peers, SENT, width), ('gy', 'gz'), split_...  8.74 us
    pallas_call x1, Pallas kernels, per_device(): pl.pallas_call(far_kernel, out_shape=[jax.ShapeDtypeStruct((peers, 12, wi...  6.32 us
    ppermute x1, starting transfers between devices, per_device(): high = lax.ppermute(region[:60], 'gx', backward)  3.83 us
    pallas_call x1, Pallas kernels, per_device(): pl.pallas_call(pack_kernel, out_shape=jax.ShapeDtypeStruct((peers * SENT,...  2.04 us
  transfers between devices with their start and end apart: 3, of which 1 were waited for; matrix products, arithmetic and copies ran while one was open for 5% of the time, Pallas kernels for 26%

profile of v7, /device:TPU:1, one launch (start us, length us, event | category | flops | bytes accessed | tf_op | source)
XLA Modules:
  0.0 80.0 jit_solution(970348187838906993)
XLA Ops:
  0.0 2.0 %shard_map.82 = f32[1792,128]{1,0:T(8,128)} custom-call(s32[1]{0:T(128)} %bitcast.5.half_hi, s32[1]{0:T(128)} %bitcast.6.side, f32[3,128,128]{2,1,0:T(8,128)} %bitcast.83, f32[128,128]{1,0:T(8,128)} %bitcast.84, s32[128,128]{1,0:T(8,128)} %bitcast.85), custom_call_target="tpu_custom_call" | custom-call | tf_op jit(solution)/shard_map/pallas_call | solution.py:350
  2.0 0.0 copy-start.2
  2.1 0.0 copy-start.3
  2.1 0.0 copy-start.4
  2.1 0.0 copy-start.1
  2.1 0.0 copy-start
  2.1 8.7 %all-to-all-start = ((f32[32,56,128]{2,1,0:T(8,128)}), f32[32,56,128]{2,1,0:T(8,128)S(1)}, u32[]{:S(2)}, u32[]{:S(2)}) async-start(f32[32,56,128]{2,1,0:T(8,128)} %bitcast.81), calls=%async_computation | async-start | bytes 1835008 | tf_op jit(solution)/shard_map/all_to_all | solution.py:363
  10.9 0.0 copy-done.2
  10.9 0.4 fusion
  11.3 0.6 convert_reduce_fusion.1
  12.6 0.6 convert_reduce_fusion
  13.9 0.2 select_reduce_fusion.2
  14.2 0.4 select_reduce_fusion.1
  14.6 0.0 copy-done.3
  14.6 0.0 copy-done.4
  14.7 0.1 stack.174
  14.7 0.1 copy.70
  14.9 0.1 stack.160
  15.1 0.1 copy.69
  15.2 0.1 pad.15.clone
  15.3 0.7 concatenate.23
  16.0 0.1 pad_add_fusion.1.steps
  16.1 0.0 copy-done.1
  16.2 0.1 maximum_bitcast_fusion
  16.2 0.0 copy-done
  16.3 9.7 %all-to-all-done.arrived = f32[32,56,128]{2,1,0:T(8,128)S(1)} async-done(((f32[32,56,128]{2,1,0:T(8,128)}), f32[32,56,128]{2,1,0:T(8,128)S(1)}, u32[]{:S(2)}, u32[]{:S(2)}) %all-to-all-start) | async-done | bytes 917536 | tf_op jit(solution)/shard_map/all_to_all | solution.py:363
  26.0 0.2 shard_map.83.region
  26.2 3.8 %collective-permute-start.1 = (f32[60,8,128]{2,1,0:T(8,128)S(1)}, f32[60,8,128]{2,1,0:T(8,128)S(1)}, u32[]{:S(2)}, u32[]{:S(2)}) collective-permute-start(f32[60,8,128]{2,1,0:T(8,128)S(1)} %get-tuple-element.36), channel_id=1, source_target_pairs={{32,0},{64,32},{96,64},{0,96},{33,1},{65,33},{97,65},{1,97},{34,2}... | collective-permute-start | bytes 737288 | tf_op jit(solution)/shard_map/ppermute | solution.py:379
  30.0 0.0 collective-permute-start
  30.0 21.1 %shard_map.84 = (f32[129,16,128]{2,1,0:T(8,128)S(1)}, bf16[128,128,128]{2,1,0:T(8,128)(2,1)S(1)}, bf16[128,128,128]{2,1,0:T(8,128)(2,1)S(1)}) custom-call(s32[2]{0:T(128)S(1)} %pad_add_fusion.1.steps, s32[4,528]{1,0:T(4,128)S(1)} %pad_add_fusion.ids, f32[240,8,128]{2,1,0:T(8,128)S(1)} %shard_map.83.region, bf16[96,256]{1,0:T(8,128)(2,1)S(1)} %fusion.5.w_home, ...), custom_call_target="tpu_custom_call" | custom-call | flops 10000000000 | bytes 10000000 | tf_op jit(solution)/shard_map/pallas_call | solution.py:392
  51.1 0.0 collective-permute-done.1.high
  51.1 0.0 collective-permute-done.low
  51.1 6.3 %shard_map.85 = (f32[32,12,128]{2,1,0:T(8,128)S(1)}, f32[129,16,128]{2,1,0:T(8,128)S(1)}) custom-call(s32[2]{0:T(128)S(1)} %pad_add_fusion.1.steps, s32[4,528]{1,0:T(4,128)S(1)} %pad_add_fusion.ids, f32[60,8,128]{2,1,0:T(8,128)S(1)} %collective-permute-done.low, f32[60,8,128]{2,1,0:T(8,128)S(1)} %collective-permute-done.1.high, ...), custom_call_target="tpu_custom_call", output_to_operand_aliasing={{1}: (8, {})} | custom-call | tf_op jit(solution)/shard_map/pallas_call | solution.py:401
  57.5 21.8 %all_to_all.10 = f32[32,12,128]{2,1,0:T(8,128)S(1)} all-to-all(f32[32,12,128]{2,1,0:T(8,128)S(1)} %get-tuple-element.12), channel_id=1, replica_groups=mesh['gx'=4,'gy'=4,'gz'=8] {'gy','gz'}, dimensions={0} | all-to-all | bytes 393216 | tf_op jit(solution)/shard_map/all_to_all | solution.py:410
  79.2 0.1 copy.73
  79.3 0.7 copy.74
  (25 shorter events, 0.3 us)
Async XLA Ops:
  2.0 8.8 %copy-start.2 = (s32[1,1,1,2,512]{4,3,2,1,0:T(2,128)S(1)}, s32[1,1,1,2,512]{4,3,2,1,0:T(2,128)}, u32[]{:S(2)}) copy-start(s32[1,1,1,2,512]{4,3,2,1,0:T(2,128)} %param.13) | copy-start | bytes 12292
  2.1 12.5 %copy-start.3 = (f32[64]{0:T(128)S(1)}, f32[64]{0:T(128)}, u32[]{:S(2)}) copy-start(f32[64]{0:T(128)} %param.11) | copy-start | bytes 772
  2.1 12.5 %copy-start.4 = (f32[64]{0:T(128)S(1)}, f32[64]{0:T(128)}, u32[]{:S(2)}) copy-start(f32[64]{0:T(128)} %param.12) | copy-start | bytes 772
  2.1 14.0 %copy-start.1 = (bf16[80,96]{1,0:T(8,128)(2,1)S(1)}, bf16[80,96]{1,0:T(8,128)(2,1)}, u32[]{:S(2)}) copy-start(bf16[80,96]{1,0:T(8,128)(2,1)} %constant.242) | copy-start | bytes 46084
  2.1 14.1 %copy-start = (bf16[96,128]{1,0:T(8,128)(2,1)S(1)}, bf16[96,128]{1,0:T(8,128)(2,1)}, u32[]{:S(2)}) copy-start(bf16[96,128]{1,0:T(8,128)(2,1)} %constant.243) | copy-start | bytes 73732
  2.1 23.9 %all-to-all-start = ((f32[32,56,128]{2,1,0:T(8,128)}), f32[32,56,128]{2,1,0:T(8,128)S(1)}, u32[]{:S(2)}, u32[]{:S(2)}) async-start(f32[32,56,128]{2,1,0:T(8,128)} %bitcast.81), calls=%async_computation | async-start | bytes 1835008 | tf_op jit(solution)/shard_map/all_to_all | solution.py:363
  26.2 24.9 %collective-permute-start.1 = (f32[60,8,128]{2,1,0:T(8,128)S(1)}, f32[60,8,128]{2,1,0:T(8,128)S(1)}, u32[]{:S(2)}, u32[]{:S(2)}) collective-permute-start(f32[60,8,128]{2,1,0:T(8,128)S(1)} %get-tuple-element.36), channel_id=1, source_target_pairs={{32,0},{64,32},{96,64},{0,96},{33,1},{65,33},{97,65},{1,97},{34,2}... | collective-permute-start | bytes 737288 | tf_op jit(solution)/shard_map/ppermute | solution.py:379
  30.0 21.1 %collective-permute-start = (f32[60,8,128]{2,1,0:T(8,128)S(1)}, f32[60,8,128]{2,1,0:T(8,128)S(1)}, u32[]{:S(2)}, u32[]{:S(2)}) collective-permute-start(f32[60,8,128]{2,1,0:T(8,128)S(1)} %get-tuple-element.37), channel_id=1, source_target_pairs={{0,32},{32,64},{64,96},{96,0},{1,33},{33,65},{65,97},{97,1},{2,34}... | collective-permute-start | bytes 737288 | tf_op jit(solution)/shard_map/ppermute | solution.py:378

commit v8 on v7

--- a/solution.py
+++ b/solution.py
@@ -29,6 +29,7 @@
 NY = 48
 NZ = TYPES + 32
 BATCH = 4
+SIZES = (4, 2, 1)
 GROUP = 8
 FAR_GROUP = 10
 NEAR = 240
@@ -245,12 +246,17 @@
             both(buf_a, buf_b, jnp.minimum(2 * i + 2, last), 2 * i + 1)
             return carry
 
-        def twice(i, carry):
-            body(first + 2 * i, carry)
-            return body(first + 2 * i + 1, carry)
-
-        lax.fori_loop(0, pairs // 2, twice, 0)
-        lax.fori_loop(first + pairs // 2 * 2, first + pairs, body, 0)
+        at = first
+        for size in SIZES:
+
+            def several(i, carry, size=size, at=at):
+                for k in range(size):
+                    body(at + i * size + k, carry)
+                return carry
+
+            steps = (first + pairs - at) // size
+            lax.fori_loop(0, steps, several, 0)
+            at = at + steps * size
 
 
 def near_place(b):
@@ -278,8 +284,8 @@
         store_source(places, z, w_src, rx, ry, rr)
         return carry
 
-    lax.fori_loop(0, 128 // GROUP, owned, 0, unroll=4)
-    lax.fori_loop(0, 112 // GROUP, rim, 0, unroll=7)
+    lax.fori_loop(0, 128 // GROUP, owned, 0, unroll=8)
+    lax.fori_loop(0, 112 // GROUP, rim, 0, unroll=14)
     acc[...] = jnp.zeros_like(acc)
     all_tiles(0, steps[0], ids, lx, ly, rx, ry, rr, acc, buf_a, buf_b)
 
@@ -292,7 +298,7 @@
             store_source([p + 60 * k for p in places], z, w_src, rx, ry, rr)
         return carry
 
-    lax.fori_loop(0, 60 // FAR_GROUP, prepare, 0, unroll=2)
+    lax.fori_loop(0, 60 // FAR_GROUP, prepare, 0, unroll=6)
     all_tiles(steps[0], steps[1], ids, lx, ly, rx, ry, rr, acc_out, buf_a, buf_b)
 
     def finish(s, carry):

time: 80.1 us -> 76.2 us (0.951)
  Pallas kernels: 29.6 us -> 25.1 us
    pallas_call x1, Pallas kernels: 21.1 us -> 17.1 us  [per_device(): pl.pallas_call(near_kernel, out_shape=[acc_shape, factor_shape, factor_sh...]
  transfers between devices with their start and end apart: 3 -> 3, of which waited for: 1 -> 1; matrix products, arithmetic and copies ran while one was open for 5% -> 5% of each run, Pallas kernels for 26% -> 23%
where the time goes in v8:
time: 76.2 us; the launch traced here: 75.6 us
  Pallas kernels  25.1 us (33%)
  blocking collectives  22 us (29%)
  starting transfers between devices  12.6 us (17%)
  waiting for transfers between devices  9.71 us (13%)
  other arithmetic  2.65 us (3%)
  local copies, waits for them, and re-layouts  2.07 us (3%)
  between operations  1.61 us (2%)
    all_to_all x1, blocking collectives, per_device(): lax.all_to_all(totals, ('gy', 'gz'), split_axis=0, concat_axis=0, tiled=T...  22 us
    pallas_call x1, Pallas kernels, per_device(): pl.pallas_call(near_kernel, out_shape=[acc_shape, factor_shape, factor_sh...  17.1 us
    all_to_all x1, waiting for transfers between devices, per_device(): lax.all_to_all(outgoing.reshape(peers, SENT, width), ('gy', 'gz'), split_...  9.71 us
    all_to_all x1, starting transfers between devices, per_device(): lax.all_to_all(outgoing.reshape(peers, SENT, width), ('gy', 'gz'), split_...  8.74 us
    pallas_call x1, Pallas kernels, per_device(): pl.pallas_call(far_kernel, out_shape=[jax.ShapeDtypeStruct((peers, 12, wi...  5.79 us
    ppermute x1, starting transfers between devices, per_device(): high = lax.ppermute(region[:60], 'gx', backward)  3.83 us
    pallas_call x1, Pallas kernels, per_device(): pl.pallas_call(pack_kernel, out_shape=jax.ShapeDtypeStruct((peers * SENT,...  2.04 us
  transfers between devices with their start and end apart: 3, of which 1 were waited for; matrix products, arithmetic and copies ran while one was open for 5% of the time, Pallas kernels for 23%

profile of v8, /device:TPU:1, one launch (start us, length us, event | category | flops | bytes accessed | tf_op | source)
XLA Modules:
  0.0 75.6 jit_solution(2967821910844529090)
XLA Ops:
  0.0 2.0 %shard_map.82 = f32[1792,128]{1,0:T(8,128)} custom-call(s32[1]{0:T(128)} %bitcast.5.half_hi, s32[1]{0:T(128)} %bitcast.6.side, f32[3,128,128]{2,1,0:T(8,128)} %bitcast.83, f32[128,128]{1,0:T(8,128)} %bitcast.84, s32[128,128]{1,0:T(8,128)} %bitcast.85), custom_call_target="tpu_custom_call" | custom-call | tf_op jit(solution)/shard_map/pallas_call | solution.py:356
  2.0 0.0 copy-start.2
  2.1 0.0 copy-start.3
  2.1 0.0 copy-start.4
  2.1 0.0 copy-start.1
  2.1 0.0 copy-start
  2.1 8.7 %all-to-all-start = ((f32[32,56,128]{2,1,0:T(8,128)}), f32[32,56,128]{2,1,0:T(8,128)S(1)}, u32[]{:S(2)}, u32[]{:S(2)}) async-start(f32[32,56,128]{2,1,0:T(8,128)} %bitcast.81), calls=%async_computation | async-start | bytes 1835008 | tf_op jit(solution)/shard_map/all_to_all | solution.py:369
  10.9 0.0 copy-done.2
  10.9 0.4 fusion
  11.3 0.6 convert_reduce_fusion.1
  12.6 0.6 convert_reduce_fusion
  13.9 0.2 select_reduce_fusion.2
  14.2 0.4 select_reduce_fusion.1
  14.6 0.0 copy-done.3
  14.6 0.0 copy-done.4
  14.7 0.1 stack.174
  14.7 0.1 copy.70
  14.9 0.1 stack.160
  15.1 0.1 copy.69
  15.2 0.1 pad.15.clone
  15.3 0.7 concatenate.23
  16.0 0.1 pad_add_fusion.1.steps
  16.1 0.0 copy-done.1
  16.2 0.1 maximum_bitcast_fusion
  16.2 0.0 copy-done
  16.3 9.7 %all-to-all-done.arrived = f32[32,56,128]{2,1,0:T(8,128)S(1)} async-done(((f32[32,56,128]{2,1,0:T(8,128)}), f32[32,56,128]{2,1,0:T(8,128)S(1)}, u32[]{:S(2)}, u32[]{:S(2)}) %all-to-all-start) | async-done | bytes 917536 | tf_op jit(solution)/shard_map/all_to_all | solution.py:369
  26.0 0.2 shard_map.83.region
  26.2 3.8 %collective-permute-start.1 = (f32[60,8,128]{2,1,0:T(8,128)S(1)}, f32[60,8,128]{2,1,0:T(8,128)S(1)}, u32[]{:S(2)}, u32[]{:S(2)}) collective-permute-start(f32[60,8,128]{2,1,0:T(8,128)S(1)} %get-tuple-element.36), channel_id=1, source_target_pairs={{32,0},{64,32},{96,64},{0,96},{33,1},{65,33},{97,65},{1,97},{34,2}... | collective-permute-start | bytes 737288 | tf_op jit(solution)/shard_map/ppermute | solution.py:385
  30.0 0.0 collective-permute-start
  30.0 17.1 %shard_map.84 = (f32[129,16,128]{2,1,0:T(8,128)S(1)}, bf16[128,128,128]{2,1,0:T(8,128)(2,1)S(1)}, bf16[128,128,128]{2,1,0:T(8,128)(2,1)S(1)}) custom-call(s32[2]{0:T(128)S(1)} %pad_add_fusion.1.steps, s32[4,528]{1,0:T(4,128)S(1)} %pad_add_fusion.ids, f32[240,8,128]{2,1,0:T(8,128)S(1)} %shard_map.83.region, bf16[96,256]{1,0:T(8,128)(2,1)S(1)} %fusion.5.w_home, ...), custom_call_target="tpu_custom_call" | custom-call | flops 10000000000 | bytes 10000000 | tf_op jit(solution)/shard_map/pallas_call | solution.py:398
  47.1 0.0 collective-permute-done.1.high
  47.1 0.0 collective-permute-done.low
  47.1 5.8 %shard_map.85 = (f32[32,12,128]{2,1,0:T(8,128)S(1)}, f32[129,16,128]{2,1,0:T(8,128)S(1)}) custom-call(s32[2]{0:T(128)S(1)} %pad_add_fusion.1.steps, s32[4,528]{1,0:T(4,128)S(1)} %pad_add_fusion.ids, f32[60,8,128]{2,1,0:T(8,128)S(1)} %collective-permute-done.low, f32[60,8,128]{2,1,0:T(8,128)S(1)} %collective-permute-done.1.high, ...), custom_call_target="tpu_custom_call", output_to_operand_aliasing={{1}: (8, {})} | custom-call | tf_op jit(solution)/shard_map/pallas_call | solution.py:407
  52.9 22.0 %all_to_all.10 = f32[32,12,128]{2,1,0:T(8,128)S(1)} all-to-all(f32[32,12,128]{2,1,0:T(8,128)S(1)} %get-tuple-element.12), channel_id=1, replica_groups=mesh['gx'=4,'gy'=4,'gz'=8] {'gy','gz'}, dimensions={0} | all-to-all | bytes 393216 | tf_op jit(solution)/shard_map/all_to_all | solution.py:416
  74.9 0.1 copy.73
  74.9 0.7 copy.74
  (25 shorter events, 0.3 us)
Async XLA Ops:
  2.0 8.8 %copy-start.2 = (s32[1,1,1,2,512]{4,3,2,1,0:T(2,128)S(1)}, s32[1,1,1,2,512]{4,3,2,1,0:T(2,128)}, u32[]{:S(2)}) copy-start(s32[1,1,1,2,512]{4,3,2,1,0:T(2,128)} %param.13) | copy-start | bytes 12292
  2.1 12.5 %copy-start.3 = (f32[64]{0:T(128)S(1)}, f32[64]{0:T(128)}, u32[]{:S(2)}) copy-start(f32[64]{0:T(128)} %param.11) | copy-start | bytes 772
  2.1 12.5 %copy-start.4 = (f32[64]{0:T(128)S(1)}, f32[64]{0:T(128)}, u32[]{:S(2)}) copy-start(f32[64]{0:T(128)} %param.12) | copy-start | bytes 772
  2.1 14.0 %copy-start.1 = (bf16[80,96]{1,0:T(8,128)(2,1)S(1)}, bf16[80,96]{1,0:T(8,128)(2,1)}, u32[]{:S(2)}) copy-start(bf16[80,96]{1,0:T(8,128)(2,1)} %constant.242) | copy-start | bytes 46084
  2.1 14.1 %copy-start = (bf16[96,128]{1,0:T(8,128)(2,1)S(1)}, bf16[96,128]{1,0:T(8,128)(2,1)}, u32[]{:S(2)}) copy-start(bf16[96,128]{1,0:T(8,128)(2,1)} %constant.243) | copy-start | bytes 73732
  2.1 23.9 %all-to-all-start = ((f32[32,56,128]{2,1,0:T(8,128)}), f32[32,56,128]{2,1,0:T(8,128)S(1)}, u32[]{:S(2)}, u32[]{:S(2)}) async-start(f32[32,56,128]{2,1,0:T(8,128)} %bitcast.81), calls=%async_computation | async-start | bytes 1835008 | tf_op jit(solution)/shard_map/all_to_all | solution.py:369
  26.2 20.9 %collective-permute-start.1 = (f32[60,8,128]{2,1,0:T(8,128)S(1)}, f32[60,8,128]{2,1,0:T(8,128)S(1)}, u32[]{:S(2)}, u32[]{:S(2)}) collective-permute-start(f32[60,8,128]{2,1,0:T(8,128)S(1)} %get-tuple-element.36), channel_id=1, source_target_pairs={{32,0},{64,32},{96,64},{0,96},{33,1},{65,33},{97,65},{1,97},{34,2}... | collective-permute-start | bytes 737288 | tf_op jit(solution)/shard_map/ppermute | solution.py:385
  30.0 17.1 %collective-permute-start = (f32[60,8,128]{2,1,0:T(8,128)S(1)}, f32[60,8,128]{2,1,0:T(8,128)S(1)}, u32[]{:S(2)}, u32[]{:S(2)}) collective-permute-start(f32[60,8,128]{2,1,0:T(8,128)S(1)} %get-tuple-element.37), channel_id=1, source_target_pairs={{0,32},{32,64},{64,96},{96,0},{1,33},{33,65},{65,97},{97,1},{2,34}... | collective-permute-start | bytes 737288 | tf_op jit(solution)/shard_map/ppermute | solution.py:384
